TPU v7x, 32 devices: a whole 2x2x4 slice. The times are simulated.
32 devices in a mesh: space: 8 (over z, x), sub: 4 (over y, core).
Axes of the slice: x: 2, y: 2, z: 4, core: 2. Of those that a mesh axis runs over, the one named last changes fastest.
Arguments:
- offsets: float32 [8, 4, 8, 4, 4, 3, 128], P('space', 'sub'), may hold values from 0.5 to 7.5
- normals: float32 [8, 4, 8, 4, 4, 3, 128], P('space', 'sub'), may hold values from -6 to 6
- density: float32 [8, 4, 8, 4, 4, 128], P('space', 'sub'), may hold values from 0.3 to 3
- tile_brick: int32 [8, 4, 8, 4, 4], P('space', 'sub'), may hold values from 0 to 63
- tile_count: int32 [8, 4, 8, 4, 4], P('space', 'sub'), may hold values from 32 to 128, as said below
Outputs:
- indicator: float32 [128, 64, 128], P('space', 'sub')
- density_field: float32 [128, 64, 128], P('space', 'sub')
Inputs may be any that keep to these rules, and one draw needn't show every extreme that they name: `tile_count`: slots at and beyond a tile's count are padding; some tile holds 128 live points.
All inputs are finite; a program needn't handle non-finite values.
Results may differ from a plain program's by a relative error of at most 0.0003.
Values sent between devices are 32-bit elements; how exact they have to be, the bound alone decides.
A program may use at most 192 MiB of HBM per device.

v0:
```python
import math

import jax
import jax.numpy as jnp
from jax import lax
from jax.sharding import PartitionSpec as P

BRICK = 8
CX = 16
CY = 16
CZ = 128
LEVELS = 4
SWEEPS = 2
COARSE = 8


screen_weight = 0.05
relax_weight = 0.8


def with_halo(x, sides, width):
    for axis, dim in sides:
        devices, length = (lax.axis_size(axis), x.shape[dim])
        up = [(i, (i + 1) % devices) for i in range(devices - 1)]
        down = [(j, i) for i, j in up]
        last = lax.slice_in_dim(x, length - width, length, axis=dim)
        first = lax.slice_in_dim(x, 0, width, axis=dim)
        before = lax.ppermute(last, axis, up)
        after = lax.ppermute(first, axis, down)
        x = jnp.concatenate([before, x, after], axis=dim)
    return x


def splat_tiles(offsets_tile, samples_tile):
    tile_total = offsets_tile.shape[0]
    slot_total = offsets_tile.shape[2]
    centers = jnp.arange(BRICK, dtype=jnp.float32) + 0.5
    weights = jnp.maximum(
        0.0, 1.0 - jnp.abs(offsets_tile[:, :, None, :] - centers[None, None, :, None])
    )
    planar = (weights[:, 0, :, None, :] * weights[:, 1, None, :, :]).reshape(
        tile_total, BRICK * BRICK, slot_total
    )
    loaded = (samples_tile[:, :, None, :] * weights[:, 2][:, None, :, :]).reshape(
        tile_total, 4 * BRICK, slot_total
    )
    result = jnp.einsum("tas,tbs->tab", planar, loaded, precision=lax.Precision.HIGHEST)
    return result.reshape(tile_total, -1)


def splat_blocks(offsets_flat, samples_flat):
    tile_total = offsets_flat.shape[0]
    block_size = math.gcd(tile_total, 64)
    slot_total = offsets_flat.shape[2]

    def one_block(inputs):
        return splat_tiles(inputs[0], inputs[1])

    result = lax.map(
        one_block,
        (
            offsets_flat.reshape(tile_total // block_size, block_size, 3, slot_total),
            samples_flat.reshape(tile_total // block_size, block_size, 4, slot_total),
        ),
    )
    return result.reshape(tile_total, -1)


def to_grid(sums):
    shaped = sums.reshape(CX // BRICK, CY // BRICK, CZ // BRICK, BRICK, BRICK, 4, BRICK)
    return shaped.transpose(5, 0, 3, 1, 4, 2, 6).reshape(4, CX, CY, CZ)


def neighbours(padded):
    total = padded[2:, 1:-1, 1:-1] + padded[:-2, 1:-1, 1:-1]
    total = total + padded[1:-1, 2:, 1:-1] + padded[1:-1, :-2, 1:-1]
    return total + padded[1:-1, 1:-1, 2:] + padded[1:-1, 1:-1, :-2]


def operate(padded, field, screen, level_index):
    return (6.0 * field - neighbours(padded)) * 0.25**level_index + screen * field


def pad_shared(field):
    rimmed = with_halo(field, (("space", 0), ("sub", 1)), 1)
    return jnp.pad(rimmed, ((0, 0), (0, 0), (1, 1)))


def sweep(padded, field, forcing, screen, diagonal, level_index):
    return field + relax_weight * (forcing - operate(padded, field, screen, level_index)) / diagonal


def restrict(field):
    sx, sy, sz = field.shape
    return field.reshape(sx // 2, 2, sy // 2, 2, sz // 2, 2).mean(axis=(1, 3, 5))


def prolong(field):
    return jnp.repeat(jnp.repeat(jnp.repeat(field, 2, axis=0), 2, axis=1), 2, axis=2)


def single_action(field, action, forcing, screen, diagonal, level_index):
    padded = pad_shared(field)
    if action == "residual":
        return (field, forcing - operate(padded, field, screen, level_index))
    return (sweep(padded, field, forcing, screen, diagonal, level_index), None)


def apply_actions(field, actions, forcing, screen, diagonal, level_index):
    residual = None
    position = 0
    while position < len(actions):
        field, residual = single_action(
            field, actions[position], forcing, screen, diagonal, level_index
        )
        position = position + 1
    return (field, residual)


def coarsest_solve(forcing, screen, level_index):
    diagonal = 6.0 * 0.25**level_index + screen
    field = relax_weight * forcing / diagonal
    field, unused = apply_actions(
        field, ["sweep"] * (COARSE - 1), forcing, screen, diagonal, level_index
    )
    return field


def vcycle(forcing, level_index, screens):
    screen = screens[level_index]
    if level_index == LEVELS - 1:
        return coarsest_solve(forcing, screen, level_index)
    diagonal = 6.0 * 0.25**level_index + screen
    field = relax_weight * forcing / diagonal
    field, residual = apply_actions(
        field, ["sweep"] * (SWEEPS - 1) + ["residual"], forcing, screen, diagonal, level_index
    )
    correction = vcycle(restrict(residual), level_index + 1, screens)
    field = field + prolong(correction)
    field, unused = apply_actions(field, ["sweep"] * SWEEPS, forcing, screen, diagonal, level_index)
    return field


def on_device(offsets, normals, density, tile_brick, tile_count):
    space_count = lax.axis_size("space")
    sub_count = lax.axis_size("sub")
    tiles_each = offsets.shape[4]
    slot_total = offsets.shape[6]
    brick_total = CX // BRICK * (CY // BRICK) * (CZ // BRICK)
    offsets_local = offsets.reshape(space_count, sub_count, tiles_each, 3, slot_total)
    samples = jnp.concatenate(
        [
            normals.reshape(space_count, sub_count, tiles_each, 3, slot_total),
            density.reshape(space_count, sub_count, tiles_each, 1, slot_total),
        ],
        axis=3,
    )
    slot_numbers = lax.broadcasted_iota(
        jnp.int32, (space_count, sub_count, tiles_each, slot_total), 3
    )
    live_slots = (
        slot_numbers < tile_count.reshape(space_count, sub_count, tiles_each)[..., None]
    ).astype(jnp.float32)
    samples = samples * live_slots[:, :, :, None, :]
    brick_ids = tile_brick.reshape(space_count, sub_count, tiles_each).astype(jnp.float32)
    partials_out = splat_blocks(
        offsets_local.reshape(-1, 3, slot_total), samples.reshape(-1, 4, slot_total)
    )
    partials_out = partials_out.reshape(space_count, sub_count, tiles_each, -1)
    partials_in, brick_in = (
        lax.all_to_all(
            lax.all_to_all(partials_out, "space", split_axis=0, concat_axis=0, tiled=True),
            "sub",
            split_axis=1,
            concat_axis=1,
            tiled=True,
        ),
        lax.all_to_all(
            lax.all_to_all(brick_ids, "space", split_axis=0, concat_axis=0, tiled=True),
            "sub",
            split_axis=1,
            concat_axis=1,
            tiled=True,
        ),
    )
    partials = partials_in.reshape(space_count * sub_count * tiles_each, -1)
    brick_numbers = jnp.arange(brick_total, dtype=jnp.float32)
    onehot = (brick_in.reshape(-1)[None, :] == brick_numbers[:, None]).astype(jnp.float32)
    sums = jnp.dot(
        onehot, partials, precision=lax.Precision.HIGHEST, preferred_element_type=jnp.float32
    )
    grid = to_grid(sums)
    density_field = grid[3]
    padded_x = with_halo(grid[0], (("space", 0),), 1)
    padded_y = with_halo(grid[1], (("sub", 1),), 1)
    padded_z = jnp.pad(grid[2], ((0, 0), (0, 0), (1, 1)))
    change = padded_x[2:] - padded_x[:-2] + (padded_y[:, 2:] - padded_y[:, :-2])
    change = change + (padded_z[:, :, 2:] - padded_z[:, :, :-2])
    forcing = -0.5 * change
    screens = []
    rho_level = density_field
    for level_index in range(LEVELS):
        screens.append(screen_weight * rho_level)
        rho_level = restrict(rho_level) if level_index < LEVELS - 1 else rho_level
    indicator = vcycle(forcing, 0, screens)
    return (indicator, density_field)


def solution(mesh):
    placed = (
        P("space", "sub", None, None, None, None, None),
        P("space", "sub", None, None, None, None, None),
        P("space", "sub", None, None, None, None),
        P("space", "sub", None, None, None),
        P("space", "sub", None, None, None),
    )
    return jax.shard_map(
        on_device,
        mesh=mesh,
        in_specs=placed,
        out_specs=(P("space", "sub", None), P("space", "sub", None)),
        check_vma=False,
    )
```

profile of v0, /device:TPU:28, one launch (start us, length us, event | category | flops | bytes accessed | tf_op | source)
XLA Modules:
  0.0 433.3 jit_solution(14011717141904269203)
XLA Ops:
  2.0 6.0 %all-to-all-start = ((f32[8,4,4]{2,1,0:T(4,128)}), f32[8,4,4]{2,1,0:T(4,128)S(1)}, u32[]{:S(2)}, u32[]{:S(2)}) async-start(f32[8,4,4]{2,1,0:T(4,128)} %copy.198), calls=%async_computation | async-start | bytes 32768 | tf_op jit(solution)/shard_map/all_to_all | solution.py:179
  12.0 12.0 %while.10 = (s32[]{:T(128)}, f32[2,64,2048]{2,1,0:T(8,128)}, f32[2,64,3,128]{3,1,0,2:T(8,128)S(1)}, f32[2,64,4,128]{3,2,1,0:T(4,128)S(1)}, s32[]{:T(128)}) while((s32[]{:T(128)}, f32[2,64,2048]{2,1,0:T(8,128)}, f32[2,64,3,128]{3,1,0,2:T(8,128)S(1)}, f32[2,64,4,128]{3,2,1,0:T(4,128)S(1)}, s32[]{:T(128)}) %tuple.80), condition=%wide.region_1.2_spmd, body=%wide.region_0.1_spmd.sunk | while | flops 202899472 | bytes 7504017 | solution.py:59
  12.3 3.4 fusion.215
  18.3 3.4 fusion.215
  24.0 2.5 reshape_reshape.4
  26.5 6.0 %all-to-all-start.2 = ((f32[8,4,4,2048]{3,2,1,0:T(4,128)}), f32[8,4,4,2048]{3,2,1,0:T(4,128)S(1)}, u32[]{:S(2)}, u32[]{:S(2)}) async-start(f32[8,4,4,2048]{3,2,1,0:T(4,128)} %reshape_reshape.4), calls=%async_computation.2 | async-start | bytes 2097152 | tf_op jit(solution)/shard_map/all_to_all | solution.py:172
  33.2 21.8 %all-to-all-done.2 = f32[8,4,4,2048]{3,2,1,0:T(4,128)S(1)} async-done(((f32[8,4,4,2048]{3,2,1,0:T(4,128)}), f32[8,4,4,2048]{3,2,1,0:T(4,128)S(1)}, u32[]{:S(2)}, u32[]{:S(2)}) %all-to-all-start.2) | async-done | bytes 1048608 | tf_op jit(solution)/shard_map/all_to_all | solution.py:172
  55.0 3.7 all-to-all-start.1
  60.5 5.5 %all-to-all-start.3 = ((f32[8,4,4,2048]{3,2,0,1:T(4,128)}), f32[8,4,4,2048]{3,2,0,1:T(4,128)S(1)}, u32[]{:S(2)}, u32[]{:S(2)}) async-start(f32[8,4,4,2048]{3,2,0,1:T(4,128)} %copy.206), calls=%async_computation.3 | async-start | bytes 2097152 | tf_op jit(solution)/shard_map/all_to_all | solution.py:171
  66.2 12.6 %all-to-all-done.3 = f32[8,4,4,2048]{3,2,0,1:T(4,128)S(1)} async-done(((f32[8,4,4,2048]{3,2,0,1:T(4,128)}), f32[8,4,4,2048]{3,2,0,1:T(4,128)S(1)}, u32[]{:S(2)}, u32[]{:S(2)}) %all-to-all-start.3) | async-done | bytes 1048608 | tf_op jit(solution)/shard_map/all_to_all | solution.py:171
  88.9 3.6 collective-permute-start.2
  96.0 3.6 collective-permute-start.1
  99.7 3.3 collective-permute-start
  107.8 2.6 squeeze.19
  113.3 3.9 collective-permute-start.5
  117.2 2.5 collective-permute-done.5
  124.1 2.6 collective-permute-done.7
  127.1 2.7 collective-permute-start.8
  129.7 3.2 collective-permute-start.9
  132.9 3.2 collective-permute-done.9
  140.5 4.4 %reshape_squeeze.3 = f32[8,2,8,2,64,2]{5,4,3,2,1,0:T(8,128)} reshape(f32[1,2,8,2,8,16,8]{6,5,4,3,2,1,0:T(8,128)S(1)} %copy.212) | data formatting | bytes 262144 | tf_op jit(solution)/shard_map/reshape;squeeze | solution.py:95
  144.9 4.0 reduce_sum.55
  149.4 9.8 %reshape.124 = f32[8,2,8,2,64,2]{5,4,3,2,1,0:T(8,128)} reshape(f32[16,16,128]{2,1,0:T(8,128)S(1)} %fusion.32) | data formatting | bytes 262144 | tf_op jit(solution)/shard_map/reshape | solution.py:95
  159.2 4.0 reduce_sum.54
  163.2 2.6 collective-permute-start.12
  165.8 3.2 collective-permute-start.13
  169.1 3.1 collective-permute-done.13
  176.6 2.6 collective-permute-done.15
  179.4 3.9 collective-permute-start.16
  185.3 4.5 %collective-permute-done.17 = f32[1,8,64]{2,1,0:T(8,128)S(1)} collective-permute-done((f32[1,8,64]{2,1,0:T(8,128)S(1)}, f32[1,8,64]{2,1,0:T(8,128)S(1)}, u32[]{:S(2)}, u32[]{:S(2)}) %collective-permute-start.17) | collective-permute-done | bytes 2080 | tf_op jit(solution)/shard_map/ppermute | solution.py:28
  198.1 3.8 collective-permute-start.20
  203.9 4.4 %collective-permute-done.21 = f32[1,4,32]{2,1,0:T(4,128)S(1)} collective-permute-done((f32[1,4,32]{2,1,0:T(4,128)S(1)}, f32[1,4,32]{2,1,0:T(4,128)S(1)}, u32[]{:S(2)}, u32[]{:S(2)}) %collective-permute-start.21) | collective-permute-done | bytes 544 | tf_op jit(solution)/shard_map/ppermute | solution.py:28
  212.7 2.5 collective-permute-done.23
  217.3 3.9 collective-permute-start.25
  232.9 3.8 collective-permute-start.29
  236.8 2.5 collective-permute-done.29
  243.7 2.5 collective-permute-done.31
  248.3 3.9 collective-permute-start.33
  259.0 2.5 collective-permute-done.35
  263.6 3.9 collective-permute-start.37
  274.3 2.5 collective-permute-done.39
  278.9 3.9 collective-permute-start.41
  289.6 2.5 collective-permute-done.43
  294.2 3.9 collective-permute-start.45
  304.9 2.5 collective-permute-done.47
  309.5 4.1 collective-permute-start.49
  320.2 2.5 collective-permute-done.51
  324.8 3.9 collective-permute-start.53
  335.5 2.5 collective-permute-done.55
  340.4 3.9 collective-permute-start.57
  351.1 2.5 collective-permute-done.59
  355.7 3.9 collective-permute-start.61
  366.5 2.5 collective-permute-done.63
  371.4 3.9 collective-permute-start.65
  375.3 2.5 collective-permute-done.65
  382.2 2.5 collective-permute-done.67
  386.8 3.9 collective-permute-start.69
  397.6 2.5 collective-permute-done.71
  403.1 3.9 collective-permute-start.73
  407.1 2.5 collective-permute-done.73
  414.0 2.6 collective-permute-done.75
  418.9 3.9 collective-permute-start.77
  422.8 2.5 collective-permute-done.77
  429.7 2.6 collective-permute-done.79
  (274 shorter events, 184.6 us)
Async XLA Ops:
  2.0 24.4 %all-to-all-start = ((f32[8,4,4]{2,1,0:T(4,128)}), f32[8,4,4]{2,1,0:T(4,128)S(1)}, u32[]{:S(2)}, u32[]{:S(2)}) async-start(f32[8,4,4]{2,1,0:T(4,128)} %copy.198), calls=%async_computation | async-start | bytes 32768 | tf_op jit(solution)/shard_map/all_to_all | solution.py:179
  26.5 28.5 %all-to-all-start.2 = ((f32[8,4,4,2048]{3,2,1,0:T(4,128)}), f32[8,4,4,2048]{3,2,1,0:T(4,128)S(1)}, u32[]{:S(2)}, u32[]{:S(2)}) async-start(f32[8,4,4,2048]{3,2,1,0:T(4,128)} %reshape_reshape.4), calls=%async_computation.2 | async-start | bytes 2097152 | tf_op jit(solution)/shard_map/all_to_all | solution.py:172
  55.0 5.5 %all-to-all-start.1 = ((f32[8,4,4]{0,2,1:T(4,128)}), f32[8,4,4]{0,2,1:T(4,128)S(1)}, u32[]{:S(2)}, u32[]{:S(2)}) async-start(f32[8,4,4]{0,2,1:T(4,128)} %copy.199), calls=%async_computation.1 | async-start | bytes 16384 | tf_op jit(solution)/shard_map/all_to_all | solution.py:178
  60.5 18.3 %all-to-all-start.3 = ((f32[8,4,4,2048]{3,2,0,1:T(4,128)}), f32[8,4,4,2048]{3,2,0,1:T(4,128)S(1)}, u32[]{:S(2)}, u32[]{:S(2)}) async-start(f32[8,4,4,2048]{3,2,0,1:T(4,128)} %copy.206), calls=%async_computation.3 | async-start | bytes 2097152 | tf_op jit(solution)/shard_map/all_to_all | solution.py:171
  86.9 23.5 %collective-permute-start.3 = (f32[16,1,128]{2,1,0:T(1,128)}, f32[16,1,128]{2,1,0:T(1,128)S(1)}, u32[]{:S(2)}, u32[]{:S(2)}) collective-permute-start(f32[16,1,128]{2,1,0:T(1,128)} %get-tuple-element.81), channel_id=1, source_target_pairs={{0,1},{1,2},{2,3},{4,5},{5,6},{6,7},{8,9},{9,10},{10,11},{12,13},{... | collective-permute-start | bytes 24584 | tf_op jit(solution)/shard_map/ppermute | solution.py:28
  88.9 21.6 %collective-permute-start.2 = (f32[16,1,128]{2,1,0:T(1,128)}, f32[16,1,128]{2,1,0:T(1,128)S(1)}, u32[]{:S(2)}, u32[]{:S(2)}) collective-permute-start(f32[16,1,128]{2,1,0:T(1,128)} %get-tuple-element.80), channel_id=1, source_target_pairs={{1,0},{2,1},{3,2},{5,4},{6,5},{7,6},{9,8},{10,9},{11,10},{13,12},{... | collective-permute-start | bytes 24584 | tf_op jit(solution)/shard_map/ppermute | solution.py:29
  96.0 14.4 %collective-permute-start.1 = (f32[1,16,128]{2,1,0:T(8,128)}, f32[1,16,128]{2,1,0:T(8,128)}, u32[]{:S(2)}, u32[]{:S(2)}) collective-permute-start(f32[1,16,128]{2,1,0:T(8,128)} %get-tuple-element.79), channel_id=1, source_target_pairs={{0,4},{4,8},{8,12},{12,16},{16,20},{20,24},{24,28},{1,5},{5,9},{9,... | collective-permute-start | bytes 24584 | tf_op jit(solution)/shard_map/ppermute | solution.py:28
  99.7 10.8 %collective-permute-start = (f32[1,16,128]{2,1,0:T(8,128)}, f32[1,16,128]{2,1,0:T(8,128)}, u32[]{:S(2)}, u32[]{:S(2)}) collective-permute-start(f32[1,16,128]{2,1,0:T(8,128)} %get-tuple-element.78), channel_id=1, source_target_pairs={{4,0},{8,4},{12,8},{16,12},{20,16},{24,20},{28,24},{5,1},{9,5},{13... | collective-permute-start | bytes 24584 | tf_op jit(solution)/shard_map/ppermute | solution.py:29
  111.3 5.9 %collective-permute-start.4 = (f32[1,16,128]{2,1,0:T(8,128)S(1)}, f32[1,16,128]{2,1,0:T(8,128)S(1)}, u32[]{:S(2)}, u32[]{:S(2)}) collective-permute-start(f32[1,16,128]{2,1,0:T(8,128)S(1)} %get-tuple-element.77), channel_id=1, source_target_pairs={{4,0},{8,4},{12,8},{16,12},{20,16},{24,20},{28,24},{5,1},{9,5},{13... | collective-permute-start | bytes 24584 | tf_op jit(solution)/shard_map/ppermute | solution.py:29
  113.3 6.4 %collective-permute-start.5 = (f32[1,16,128]{2,1,0:T(8,128)S(1)}, f32[1,16,128]{2,1,0:T(8,128)S(1)}, u32[]{:S(2)}, u32[]{:S(2)}) collective-permute-start(f32[1,16,128]{2,1,0:T(8,128)S(1)} %get-tuple-element.76), channel_id=1, source_target_pairs={{0,4},{4,8},{8,12},{12,16},{16,20},{20,24},{24,28},{1,5},{5,9},{9,... | collective-permute-start | bytes 24584 | tf_op jit(solution)/shard_map/ppermute | solution.py:28
  121.7 5.0 %collective-permute-start.7 = (f32[18,1,128]{2,1,0:T(1,128)S(1)}, f32[18,1,128]{2,1,0:T(1,128)S(1)}, u32[]{:S(2)}, u32[]{:S(2)}) collective-permute-start(f32[18,1,128]{2,1,0:T(1,128)S(1)} %get-tuple-element.68), channel_id=1, source_target_pairs={{0,1},{1,2},{2,3},{4,5},{5,6},{6,7},{8,9},{9,10},{10,11},{12,13},{... | collective-permute-start | bytes 27656 | tf_op jit(solution)/shard_map/ppermute | solution.py:28
  127.1 5.9 %collective-permute-start.8 = (f32[1,16,128]{2,1,0:T(8,128)S(1)}, f32[1,16,128]{2,1,0:T(8,128)S(1)}, u32[]{:S(2)}, u32[]{:S(2)}) collective-permute-start(f32[1,16,128]{2,1,0:T(8,128)S(1)} %get-tuple-element.75), channel_id=1, source_target_pairs={{4,0},{8,4},{12,8},{16,12},{20,16},{24,20},{28,24},{5,1},{9,5},{13... | collective-permute-start | bytes 24584 | tf_op jit(solution)/shard_map/ppermute | solution.py:29
  129.7 6.4 %collective-permute-start.9 = (f32[1,16,128]{2,1,0:T(8,128)S(1)}, f32[1,16,128]{2,1,0:T(8,128)S(1)}, u32[]{:S(2)}, u32[]{:S(2)}) collective-permute-start(f32[1,16,128]{2,1,0:T(8,128)S(1)} %get-tuple-element.74), channel_id=1, source_target_pairs={{0,4},{4,8},{8,12},{12,16},{16,20},{20,24},{24,28},{1,5},{5,9},{9,... | collective-permute-start | bytes 24584 | tf_op jit(solution)/shard_map/ppermute | solution.py:28
  136.2 12.7 %collective-permute-start.10 = (f32[18,1,128]{2,1,0:T(1,128)S(1)}, f32[18,1,128]{2,1,0:T(1,128)S(1)}, u32[]{:S(2)}, u32[]{:S(2)}) collective-permute-start(f32[18,1,128]{2,1,0:T(1,128)S(1)} %get-tuple-element.67), channel_id=1, source_target_pairs={{1,0},{2,1},{3,2},{5,4},{6,5},{7,6},{9,8},{10,9},{11,10},{13,12},{... | collective-permute-start | bytes 27656 | tf_op jit(solution)/shard_map/ppermute | solution.py:29
  138.1 10.8 %collective-permute-start.11 = (f32[18,1,128]{2,1,0:T(1,128)S(1)}, f32[18,1,128]{2,1,0:T(1,128)S(1)}, u32[]{:S(2)}, u32[]{:S(2)}) collective-permute-start(f32[18,1,128]{2,1,0:T(1,128)S(1)} %get-tuple-element.66), channel_id=1, source_target_pairs={{0,1},{1,2},{2,3},{4,5},{5,6},{6,7},{8,9},{9,10},{10,11},{12,13},{... | collective-permute-start | bytes 27656 | tf_op jit(solution)/shard_map/ppermute | solution.py:28
  163.2 5.9 %collective-permute-start.12 = (f32[1,8,64]{2,1,0:T(8,128)S(1)}, f32[1,8,64]{2,1,0:T(8,128)S(1)}, u32[]{:S(2)}, u32[]{:S(2)}) collective-permute-start(f32[1,8,64]{2,1,0:T(8,128)S(1)} %get-tuple-element.99), channel_id=1, source_target_pairs={{4,0},{8,4},{12,8},{16,12},{20,16},{24,20},{28,24},{5,1},{9,5},{13... | collective-permute-start | bytes 6152 | tf_op jit(solution)/shard_map/ppermute | solution.py:29
  165.8 6.4 %collective-permute-start.13 = (f32[1,8,64]{2,1,0:T(8,128)S(1)}, f32[1,8,64]{2,1,0:T(8,128)S(1)}, u32[]{:S(2)}, u32[]{:S(2)}) collective-permute-start(f32[1,8,64]{2,1,0:T(8,128)S(1)} %get-tuple-element.98), channel_id=1, source_target_pairs={{0,4},{4,8},{8,12},{12,16},{16,20},{20,24},{24,28},{1,5},{5,9},{9,... | collective-permute-start | bytes 6152 | tf_op jit(solution)/shard_map/ppermute | solution.py:28
  174.2 4.9 %collective-permute-start.15 = (f32[10,1,64]{2,1,0:T(1,128)S(1)}, f32[10,1,64]{2,1,0:T(1,128)S(1)}, u32[]{:S(2)}, u32[]{:S(2)}) collective-permute-start(f32[10,1,64]{2,1,0:T(1,128)S(1)} %get-tuple-element.88), channel_id=1, source_target_pairs={{0,1},{1,2},{2,3},{4,5},{5,6},{6,7},{8,9},{9,10},{10,11},{12,13},{... | collective-permute-start | bytes 7688 | tf_op jit(solution)/shard_map/ppermute | solution.py:28
  179.4 5.9 %collective-permute-start.16 = (f32[1,8,64]{2,1,0:T(8,128)S(1)}, f32[1,8,64]{2,1,0:T(8,128)S(1)}, u32[]{:S(2)}, u32[]{:S(2)}) collective-permute-start(f32[1,8,64]{2,1,0:T(8,128)S(1)} %get-tuple-element.97), channel_id=1, source_target_pairs={{4,0},{8,4},{12,8},{16,12},{20,16},{24,20},{28,24},{5,1},{9,5},{13... | collective-permute-start | bytes 6152 | tf_op jit(solution)/shard_map/ppermute | solution.py:29
  183.3 6.4 %collective-permute-start.17 = (f32[1,8,64]{2,1,0:T(8,128)S(1)}, f32[1,8,64]{2,1,0:T(8,128)S(1)}, u32[]{:S(2)}, u32[]{:S(2)}) collective-permute-start(f32[1,8,64]{2,1,0:T(8,128)S(1)} %get-tuple-element.96), channel_id=1, source_target_pairs={{0,4},{4,8},{8,12},{12,16},{16,20},{20,24},{24,28},{1,5},{5,9},{9,... | collective-permute-start | bytes 6152 | tf_op jit(solution)/shard_map/ppermute | solution.py:28
  189.7 5.6 %collective-permute-start.18 = (f32[10,1,64]{2,1,0:T(1,128)S(1)}, f32[10,1,64]{2,1,0:T(1,128)S(1)}, u32[]{:S(2)}, u32[]{:S(2)}) collective-permute-start(f32[10,1,64]{2,1,0:T(1,128)S(1)} %get-tuple-element.87), channel_id=1, source_target_pairs={{1,0},{2,1},{3,2},{5,4},{6,5},{7,6},{9,8},{10,9},{11,10},{13,12},{... | collective-permute-start | bytes 7688 | tf_op jit(solution)/shard_map/ppermute | solution.py:29
  191.7 4.9 %collective-permute-start.19 = (f32[10,1,64]{2,1,0:T(1,128)S(1)}, f32[10,1,64]{2,1,0:T(1,128)S(1)}, u32[]{:S(2)}, u32[]{:S(2)}) collective-permute-start(f32[10,1,64]{2,1,0:T(1,128)S(1)} %get-tuple-element.86), channel_id=1, source_target_pairs={{0,1},{1,2},{2,3},{4,5},{5,6},{6,7},{8,9},{9,10},{10,11},{12,13},{... | collective-permute-start | bytes 7688 | tf_op jit(solution)/shard_map/ppermute | solution.py:28
  198.1 5.9 %collective-permute-start.20 = (f32[1,4,32]{2,1,0:T(4,128)S(1)}, f32[1,4,32]{2,1,0:T(4,128)S(1)}, u32[]{:S(2)}, u32[]{:S(2)}) collective-permute-start(f32[1,4,32]{2,1,0:T(4,128)S(1)} %get-tuple-element.117), channel_id=1, source_target_pairs={{4,0},{8,4},{12,8},{16,12},{20,16},{24,20},{28,24},{5,1},{9,5},{13... | collective-permute-start | bytes 1544 | tf_op jit(solution)/shard_map/ppermute | solution.py:29
  201.9 6.4 %collective-permute-start.21 = (f32[1,4,32]{2,1,0:T(4,128)S(1)}, f32[1,4,32]{2,1,0:T(4,128)S(1)}, u32[]{:S(2)}, u32[]{:S(2)}) collective-permute-start(f32[1,4,32]{2,1,0:T(4,128)S(1)} %get-tuple-element.116), channel_id=1, source_target_pairs={{0,4},{4,8},{8,12},{12,16},{16,20},{20,24},{24,28},{1,5},{5,9},{9,... | collective-permute-start | bytes 1544 | tf_op jit(solution)/shard_map/ppermute | solution.py:28
  210.2 4.9 %collective-permute-start.23 = (f32[6,1,32]{2,1,0:T(1,128)S(1)}, f32[6,1,32]{2,1,0:T(1,128)S(1)}, u32[]{:S(2)}, u32[]{:S(2)}) collective-permute-start(f32[6,1,32]{2,1,0:T(1,128)S(1)} %get-tuple-element.106), channel_id=1, source_target_pairs={{0,1},{1,2},{2,3},{4,5},{5,6},{6,7},{8,9},{9,10},{10,11},{12,13},{... | collective-permute-start | bytes 2312 | tf_op jit(solution)/shard_map/ppermute | solution.py:28
  215.3 5.9 %collective-permute-start.24 = (f32[1,4,32]{2,1,0:T(4,128)S(1)}, f32[1,4,32]{2,1,0:T(4,128)S(1)}, u32[]{:S(2)}, u32[]{:S(2)}) collective-permute-start(f32[1,4,32]{2,1,0:T(4,128)S(1)} %get-tuple-element.115), channel_id=1, source_target_pairs={{4,0},{8,4},{12,8},{16,12},{20,16},{24,20},{28,24},{5,1},{9,5},{13... | collective-permute-start | bytes 1544 | tf_op jit(solution)/shard_map/ppermute | solution.py:29
  217.3 6.4 %collective-permute-start.25 = (f32[1,4,32]{2,1,0:T(4,128)S(1)}, f32[1,4,32]{2,1,0:T(4,128)S(1)}, u32[]{:S(2)}, u32[]{:S(2)}) collective-permute-start(f32[1,4,32]{2,1,0:T(4,128)S(1)} %get-tuple-element.114), channel_id=1, source_target_pairs={{0,4},{4,8},{8,12},{12,16},{16,20},{20,24},{24,28},{1,5},{5,9},{9,... | collective-permute-start | bytes 1544 | tf_op jit(solution)/shard_map/ppermute | solution.py:28
  225.6 4.9 %collective-permute-start.27 = (f32[6,1,32]{2,1,0:T(1,128)S(1)}, f32[6,1,32]{2,1,0:T(1,128)S(1)}, u32[]{:S(2)}, u32[]{:S(2)}) collective-permute-start(f32[6,1,32]{2,1,0:T(1,128)S(1)} %get-tuple-element.104), channel_id=1, source_target_pairs={{0,1},{1,2},{2,3},{4,5},{5,6},{6,7},{8,9},{9,10},{10,11},{12,13},{... | collective-permute-start | bytes 2312 | tf_op jit(solution)/shard_map/ppermute | solution.py:28
  230.9 5.9 %collective-permute-start.28 = (f32[1,2,16]{2,1,0:T(2,128)S(1)}, f32[1,2,16]{2,1,0:T(2,128)S(1)}, u32[]{:S(2)}, u32[]{:S(2)}) collective-permute-start(f32[1,2,16]{2,1,0:T(2,128)S(1)} %get-tuple-element.145), channel_id=1, source_target_pairs={{4,0},{8,4},{12,8},{16,12},{20,16},{24,20},{28,24},{5,1},{9,5},{13... | collective-permute-start | bytes 392 | tf_op jit(solution)/shard_map/ppermute | solution.py:29
  232.9 6.4 %collective-permute-start.29 = (f32[1,2,16]{2,1,0:T(2,128)S(1)}, f32[1,2,16]{2,1,0:T(2,128)S(1)}, u32[]{:S(2)}, u32[]{:S(2)}) collective-permute-start(f32[1,2,16]{2,1,0:T(2,128)S(1)} %get-tuple-element.144), channel_id=1, source_target_pairs={{0,4},{4,8},{8,12},{12,16},{16,20},{20,24},{24,28},{1,5},{5,9},{9,... | collective-permute-start | bytes 392 | tf_op jit(solution)/shard_map/ppermute | solution.py:28
  241.2 4.9 %collective-permute-start.31 = (f32[4,1,16]{2,1,0:T(1,128)S(1)}, f32[4,1,16]{2,1,0:T(1,128)S(1)}, u32[]{:S(2)}, u32[]{:S(2)}) collective-permute-start(f32[4,1,16]{2,1,0:T(1,128)S(1)} %get-tuple-element.130), channel_id=1, source_target_pairs={{0,1},{1,2},{2,3},{4,5},{5,6},{6,7},{8,9},{9,10},{10,11},{12,13},{... | collective-permute-start | bytes 776 | tf_op jit(solution)/shard_map/ppermute | solution.py:28
  246.3 5.9 %collective-permute-start.32 = (f32[1,2,16]{2,1,0:T(2,128)S(1)}, f32[1,2,16]{2,1,0:T(2,128)S(1)}, u32[]{:S(2)}, u32[]{:S(2)}) collective-permute-start(f32[1,2,16]{2,1,0:T(2,128)S(1)} %get-tuple-element.143), channel_id=1, source_target_pairs={{4,0},{8,4},{12,8},{16,12},{20,16},{24,20},{28,24},{5,1},{9,5},{13... | collective-permute-start | bytes 392 | tf_op jit(solution)/shard_map/ppermute | solution.py:29
  248.3 6.4 %collective-permute-start.33 = (f32[1,2,16]{2,1,0:T(2,128)S(1)}, f32[1,2,16]{2,1,0:T(2,128)S(1)}, u32[]{:S(2)}, u32[]{:S(2)}) collective-permute-start(f32[1,2,16]{2,1,0:T(2,128)S(1)} %get-tuple-element.142), channel_id=1, source_target_pairs={{0,4},{4,8},{8,12},{12,16},{16,20},{20,24},{24,28},{1,5},{5,9},{9,... | collective-permute-start | bytes 392 | tf_op jit(solution)/shard_map/ppermute | solution.py:28
  256.6 4.9 %collective-permute-start.35 = (f32[4,1,16]{2,1,0:T(1,128)S(1)}, f32[4,1,16]{2,1,0:T(1,128)S(1)}, u32[]{:S(2)}, u32[]{:S(2)}) collective-permute-start(f32[4,1,16]{2,1,0:T(1,128)S(1)} %get-tuple-element.128), channel_id=1, source_target_pairs={{0,1},{1,2},{2,3},{4,5},{5,6},{6,7},{8,9},{9,10},{10,11},{12,13},{... | collective-permute-start | bytes 776 | tf_op jit(solution)/shard_map/ppermute | solution.py:28
  261.6 5.9 %collective-permute-start.36 = (f32[1,2,16]{2,1,0:T(2,128)S(1)}, f32[1,2,16]{2,1,0:T(2,128)S(1)}, u32[]{:S(2)}, u32[]{:S(2)}) collective-permute-start(f32[1,2,16]{2,1,0:T(2,128)S(1)} %get-tuple-element.141), channel_id=1, source_target_pairs={{4,0},{8,4},{12,8},{16,12},{20,16},{24,20},{28,24},{5,1},{9,5},{13... | collective-permute-start | bytes 392 | tf_op jit(solution)/shard_map/ppermute | solution.py:29
  263.6 6.4 %collective-permute-start.37 = (f32[1,2,16]{2,1,0:T(2,128)S(1)}, f32[1,2,16]{2,1,0:T(2,128)S(1)}, u32[]{:S(2)}, u32[]{:S(2)}) collective-permute-start(f32[1,2,16]{2,1,0:T(2,128)S(1)} %get-tuple-element.140), channel_id=1, source_target_pairs={{0,4},{4,8},{8,12},{12,16},{16,20},{20,24},{24,28},{1,5},{5,9},{9,... | collective-permute-start | bytes 392 | tf_op jit(solution)/shard_map/ppermute | solution.py:28
  271.9 4.9 %collective-permute-start.39 = (f32[4,1,16]{2,1,0:T(1,128)S(1)}, f32[4,1,16]{2,1,0:T(1,128)S(1)}, u32[]{:S(2)}, u32[]{:S(2)}) collective-permute-start(f32[4,1,16]{2,1,0:T(1,128)S(1)} %get-tuple-element.126), channel_id=1, source_target_pairs={{0,1},{1,2},{2,3},{4,5},{5,6},{6,7},{8,9},{9,10},{10,11},{12,13},{... | collective-permute-start | bytes 776 | tf_op jit(solution)/shard_map/ppermute | solution.py:28
  277.0 5.9 %collective-permute-start.40 = (f32[1,2,16]{2,1,0:T(2,128)S(1)}, f32[1,2,16]{2,1,0:T(2,128)S(1)}, u32[]{:S(2)}, u32[]{:S(2)}) collective-permute-start(f32[1,2,16]{2,1,0:T(2,128)S(1)} %get-tuple-element.139), channel_id=1, source_target_pairs={{4,0},{8,4},{12,8},{16,12},{20,16},{24,20},{28,24},{5,1},{9,5},{13... | collective-permute-start | bytes 392 | tf_op jit(solution)/shard_map/ppermute | solution.py:29
  278.9 6.4 %collective-permute-start.41 = (f32[1,2,16]{2,1,0:T(2,128)S(1)}, f32[1,2,16]{2,1,0:T(2,128)S(1)}, u32[]{:S(2)}, u32[]{:S(2)}) collective-permute-start(f32[1,2,16]{2,1,0:T(2,128)S(1)} %get-tuple-element.138), channel_id=1, source_target_pairs={{0,4},{4,8},{8,12},{12,16},{16,20},{20,24},{24,28},{1,5},{5,9},{9,... | collective-permute-start | bytes 392 | tf_op jit(solution)/shard_map/ppermute | solution.py:28
  292.3 5.9 %collective-permute-start.44 = (f32[1,2,16]{2,1,0:T(2,128)S(1)}, f32[1,2,16]{2,1,0:T(2,128)S(1)}, u32[]{:S(2)}, u32[]{:S(2)}) collective-permute-start(f32[1,2,16]{2,1,0:T(2,128)S(1)} %get-tuple-element.137), channel_id=1, source_target_pairs={{4,0},{8,4},{12,8},{16,12},{20,16},{24,20},{28,24},{5,1},{9,5},{13... | collective-permute-start | bytes 392 | tf_op jit(solution)/shard_map/ppermute | solution.py:29
  294.2 6.4 %collective-permute-start.45 = (f32[1,2,16]{2,1,0:T(2,128)S(1)}, f32[1,2,16]{2,1,0:T(2,128)S(1)}, u32[]{:S(2)}, u32[]{:S(2)}) collective-permute-start(f32[1,2,16]{2,1,0:T(2,128)S(1)} %get-tuple-element.136), channel_id=1, source_target_pairs={{0,4},{4,8},{8,12},{12,16},{16,20},{20,24},{24,28},{1,5},{5,9},{9,... | collective-permute-start | bytes 392 | tf_op jit(solution)/shard_map/ppermute | solution.py:28
  307.6 6.1 %collective-permute-start.48 = (f32[1,2,16]{2,1,0:T(2,128)S(1)}, f32[1,2,16]{2,1,0:T(2,128)S(1)}, u32[]{:S(2)}, u32[]{:S(2)}) collective-permute-start(f32[1,2,16]{2,1,0:T(2,128)S(1)} %get-tuple-element.135), channel_id=1, source_target_pairs={{4,0},{8,4},{12,8},{16,12},{20,16},{24,20},{28,24},{5,1},{9,5},{13... | collective-permute-start | bytes 392 | tf_op jit(solution)/shard_map/ppermute | solution.py:29
  309.5 6.4 %collective-permute-start.49 = (f32[1,2,16]{2,1,0:T(2,128)S(1)}, f32[1,2,16]{2,1,0:T(2,128)S(1)}, u32[]{:S(2)}, u32[]{:S(2)}) collective-permute-start(f32[1,2,16]{2,1,0:T(2,128)S(1)} %get-tuple-element.134), channel_id=1, source_target_pairs={{0,4},{4,8},{8,12},{12,16},{16,20},{20,24},{24,28},{1,5},{5,9},{9,... | collective-permute-start | bytes 392 | tf_op jit(solution)/shard_map/ppermute | solution.py:28
  317.8 4.9 %collective-permute-start.51 = (f32[4,1,16]{2,1,0:T(1,128)S(1)}, f32[4,1,16]{2,1,0:T(1,128)S(1)}, u32[]{:S(2)}, u32[]{:S(2)}) collective-permute-start(f32[4,1,16]{2,1,0:T(1,128)S(1)} %get-tuple-element.120), channel_id=1, source_target_pairs={{0,1},{1,2},{2,3},{4,5},{5,6},{6,7},{8,9},{9,10},{10,11},{12,13},{... | collective-permute-start | bytes 776 | tf_op jit(solution)/shard_map/ppermute | solution.py:28
  322.9 5.9 %collective-permute-start.52 = (f32[1,2,16]{2,1,0:T(2,128)S(1)}, f32[1,2,16]{2,1,0:T(2,128)S(1)}, u32[]{:S(2)}, u32[]{:S(2)}) collective-permute-start(f32[1,2,16]{2,1,0:T(2,128)S(1)} %get-tuple-element.133), channel_id=1, source_target_pairs={{4,0},{8,4},{12,8},{16,12},{20,16},{24,20},{28,24},{5,1},{9,5},{13... | collective-permute-start | bytes 392 | tf_op jit(solution)/shard_map/ppermute | solution.py:29
  324.8 6.4 %collective-permute-start.53 = (f32[1,2,16]{2,1,0:T(2,128)S(1)}, f32[1,2,16]{2,1,0:T(2,128)S(1)}, u32[]{:S(2)}, u32[]{:S(2)}) collective-permute-start(f32[1,2,16]{2,1,0:T(2,128)S(1)} %get-tuple-element.132), channel_id=1, source_target_pairs={{0,4},{4,8},{8,12},{12,16},{16,20},{20,24},{24,28},{1,5},{5,9},{9,... | collective-permute-start | bytes 392 | tf_op jit(solution)/shard_map/ppermute | solution.py:28
  338.5 5.9 %collective-permute-start.56 = (f32[1,4,32]{2,1,0:T(4,128)S(1)}, f32[1,4,32]{2,1,0:T(4,128)S(1)}, u32[]{:S(2)}, u32[]{:S(2)}) collective-permute-start(f32[1,4,32]{2,1,0:T(4,128)S(1)} %get-tuple-element.111), channel_id=1, source_target_pairs={{4,0},{8,4},{12,8},{16,12},{20,16},{24,20},{28,24},{5,1},{9,5},{13... | collective-permute-start | bytes 1544 | tf_op jit(solution)/shard_map/ppermute | solution.py:29
  340.4 6.4 %collective-permute-start.57 = (f32[1,4,32]{2,1,0:T(4,128)S(1)}, f32[1,4,32]{2,1,0:T(4,128)S(1)}, u32[]{:S(2)}, u32[]{:S(2)}) collective-permute-start(f32[1,4,32]{2,1,0:T(4,128)S(1)} %get-tuple-element.110), channel_id=1, source_target_pairs={{0,4},{4,8},{8,12},{12,16},{16,20},{20,24},{24,28},{1,5},{5,9},{9,... | collective-permute-start | bytes 1544 | tf_op jit(solution)/shard_map/ppermute | solution.py:28
  348.7 4.9 %collective-permute-start.59 = (f32[6,1,32]{2,1,0:T(1,128)S(1)}, f32[6,1,32]{2,1,0:T(1,128)S(1)}, u32[]{:S(2)}, u32[]{:S(2)}) collective-permute-start(f32[6,1,32]{2,1,0:T(1,128)S(1)} %get-tuple-element.102), channel_id=1, source_target_pairs={{0,1},{1,2},{2,3},{4,5},{5,6},{6,7},{8,9},{9,10},{10,11},{12,13},{... | collective-permute-start | bytes 2312 | tf_op jit(solution)/shard_map/ppermute | solution.py:28
  353.8 5.9 %collective-permute-start.60 = (f32[1,4,32]{2,1,0:T(4,128)S(1)}, f32[1,4,32]{2,1,0:T(4,128)S(1)}, u32[]{:S(2)}, u32[]{:S(2)}) collective-permute-start(f32[1,4,32]{2,1,0:T(4,128)S(1)} %get-tuple-element.109), channel_id=1, source_target_pairs={{4,0},{8,4},{12,8},{16,12},{20,16},{24,20},{28,24},{5,1},{9,5},{13... | collective-permute-start | bytes 1544 | tf_op jit(solution)/shard_map/ppermute | solution.py:29
  355.7 6.4 %collective-permute-start.61 = (f32[1,4,32]{2,1,0:T(4,128)S(1)}, f32[1,4,32]{2,1,0:T(4,128)S(1)}, u32[]{:S(2)}, u32[]{:S(2)}) collective-permute-start(f32[1,4,32]{2,1,0:T(4,128)S(1)} %get-tuple-element.108), channel_id=1, source_target_pairs={{0,4},{4,8},{8,12},{12,16},{16,20},{20,24},{24,28},{1,5},{5,9},{9,... | collective-permute-start | bytes 1544 | tf_op jit(solution)/shard_map/ppermute | solution.py:28
  364.0 4.9 %collective-permute-start.63 = (f32[6,1,32]{2,1,0:T(1,128)S(1)}, f32[6,1,32]{2,1,0:T(1,128)S(1)}, u32[]{:S(2)}, u32[]{:S(2)}) collective-permute-start(f32[6,1,32]{2,1,0:T(1,128)S(1)} %get-tuple-element.100), channel_id=1, source_target_pairs={{0,1},{1,2},{2,3},{4,5},{5,6},{6,7},{8,9},{9,10},{10,11},{12,13},{... | collective-permute-start | bytes 2312 | tf_op jit(solution)/shard_map/ppermute | solution.py:28
  369.5 5.9 %collective-permute-start.64 = (f32[1,8,64]{2,1,0:T(8,128)S(1)}, f32[1,8,64]{2,1,0:T(8,128)S(1)}, u32[]{:S(2)}, u32[]{:S(2)}) collective-permute-start(f32[1,8,64]{2,1,0:T(8,128)S(1)} %get-tuple-element.93), channel_id=1, source_target_pairs={{4,0},{8,4},{12,8},{16,12},{20,16},{24,20},{28,24},{5,1},{9,5},{13... | collective-permute-start | bytes 6152 | tf_op jit(solution)/shard_map/ppermute | solution.py:29
  371.4 6.4 %collective-permute-start.65 = (f32[1,8,64]{2,1,0:T(8,128)S(1)}, f32[1,8,64]{2,1,0:T(8,128)S(1)}, u32[]{:S(2)}, u32[]{:S(2)}) collective-permute-start(f32[1,8,64]{2,1,0:T(8,128)S(1)} %get-tuple-element.92), channel_id=1, source_target_pairs={{0,4},{4,8},{8,12},{12,16},{16,20},{20,24},{24,28},{1,5},{5,9},{9,... | collective-permute-start | bytes 6152 | tf_op jit(solution)/shard_map/ppermute | solution.py:28
  379.7 4.9 %collective-permute-start.67 = (f32[10,1,64]{2,1,0:T(1,128)S(1)}, f32[10,1,64]{2,1,0:T(1,128)S(1)}, u32[]{:S(2)}, u32[]{:S(2)}) collective-permute-start(f32[10,1,64]{2,1,0:T(1,128)S(1)} %get-tuple-element.84), channel_id=1, source_target_pairs={{0,1},{1,2},{2,3},{4,5},{5,6},{6,7},{8,9},{9,10},{10,11},{12,13},{... | collective-permute-start | bytes 7688 | tf_op jit(solution)/shard_map/ppermute | solution.py:28
  384.9 5.9 %collective-permute-start.68 = (f32[1,8,64]{2,1,0:T(8,128)S(1)}, f32[1,8,64]{2,1,0:T(8,128)S(1)}, u32[]{:S(2)}, u32[]{:S(2)}) collective-permute-start(f32[1,8,64]{2,1,0:T(8,128)S(1)} %get-tuple-element.91), channel_id=1, source_target_pairs={{4,0},{8,4},{12,8},{16,12},{20,16},{24,20},{28,24},{5,1},{9,5},{13... | collective-permute-start | bytes 6152 | tf_op jit(solution)/shard_map/ppermute | solution.py:29
  386.8 6.4 %collective-permute-start.69 = (f32[1,8,64]{2,1,0:T(8,128)S(1)}, f32[1,8,64]{2,1,0:T(8,128)S(1)}, u32[]{:S(2)}, u32[]{:S(2)}) collective-permute-start(f32[1,8,64]{2,1,0:T(8,128)S(1)} %get-tuple-element.90), channel_id=1, source_target_pairs={{0,4},{4,8},{8,12},{12,16},{16,20},{20,24},{24,28},{1,5},{5,9},{9,... | collective-permute-start | bytes 6152 | tf_op jit(solution)/shard_map/ppermute | solution.py:28
  395.2 4.9 %collective-permute-start.71 = (f32[10,1,64]{2,1,0:T(1,128)S(1)}, f32[10,1,64]{2,1,0:T(1,128)S(1)}, u32[]{:S(2)}, u32[]{:S(2)}) collective-permute-start(f32[10,1,64]{2,1,0:T(1,128)S(1)} %get-tuple-element.82), channel_id=1, source_target_pairs={{0,1},{1,2},{2,3},{4,5},{5,6},{6,7},{8,9},{9,10},{10,11},{12,13},{... | collective-permute-start | bytes 7688 | tf_op jit(solution)/shard_map/ppermute | solution.py:28
  401.2 5.9 %collective-permute-start.72 = (f32[1,16,128]{2,1,0:T(8,128)S(1)}, f32[1,16,128]{2,1,0:T(8,128)S(1)}, u32[]{:S(2)}, u32[]{:S(2)}) collective-permute-start(f32[1,16,128]{2,1,0:T(8,128)S(1)} %get-tuple-element.73), channel_id=1, source_target_pairs={{4,0},{8,4},{12,8},{16,12},{20,16},{24,20},{28,24},{5,1},{9,5},{13... | collective-permute-start | bytes 24584 | tf_op jit(solution)/shard_map/ppermute | solution.py:29
  403.1 6.4 %collective-permute-start.73 = (f32[1,16,128]{2,1,0:T(8,128)S(1)}, f32[1,16,128]{2,1,0:T(8,128)S(1)}, u32[]{:S(2)}, u32[]{:S(2)}) collective-permute-start(f32[1,16,128]{2,1,0:T(8,128)S(1)} %get-tuple-element.72), channel_id=1, source_target_pairs={{0,4},{4,8},{8,12},{12,16},{16,20},{20,24},{24,28},{1,5},{5,9},{9,... | collective-permute-start | bytes 24584 | tf_op jit(solution)/shard_map/ppermute | solution.py:28
  411.5 5.0 %collective-permute-start.75 = (f32[18,1,128]{2,1,0:T(1,128)S(1)}, f32[18,1,128]{2,1,0:T(1,128)S(1)}, u32[]{:S(2)}, u32[]{:S(2)}) collective-permute-start(f32[18,1,128]{2,1,0:T(1,128)S(1)} %get-tuple-element.64), channel_id=1, source_target_pairs={{0,1},{1,2},{2,3},{4,5},{5,6},{6,7},{8,9},{9,10},{10,11},{12,13},{... | collective-permute-start | bytes 27656 | tf_op jit(solution)/shard_map/ppermute | solution.py:28
  416.9 5.9 %collective-permute-start.76 = (f32[1,16,128]{2,1,0:T(8,128)S(1)}, f32[1,16,128]{2,1,0:T(8,128)S(1)}, u32[]{:S(2)}, u32[]{:S(2)}) collective-permute-start(f32[1,16,128]{2,1,0:T(8,128)S(1)} %get-tuple-element.71), channel_id=1, source_target_pairs={{4,0},{8,4},{12,8},{16,12},{20,16},{24,20},{28,24},{5,1},{9,5},{13... | collective-permute-start | bytes 24584 | tf_op jit(solution)/shard_map/ppermute | solution.py:29
  418.9 6.4 %collective-permute-start.77 = (f32[1,16,128]{2,1,0:T(8,128)S(1)}, f32[1,16,128]{2,1,0:T(8,128)S(1)}, u32[]{:S(2)}, u32[]{:S(2)}) collective-permute-start(f32[1,16,128]{2,1,0:T(8,128)S(1)} %get-tuple-element.70), channel_id=1, source_target_pairs={{0,4},{4,8},{8,12},{12,16},{16,20},{20,24},{24,28},{1,5},{5,9},{9,... | collective-permute-start | bytes 24584 | tf_op jit(solution)/shard_map/ppermute | solution.py:28
  427.3 5.0 %collective-permute-start.79 = (f32[18,1,128]{2,1,0:T(1,128)S(1)}, f32[18,1,128]{2,1,0:T(1,128)S(1)}, u32[]{:S(2)}, u32[]{:S(2)}) collective-permute-start(f32[18,1,128]{2,1,0:T(1,128)S(1)} %get-tuple-element.62), channel_id=1, source_target_pairs={{0,1},{1,2},{2,3},{4,5},{5,6},{6,7},{8,9},{9,10},{10,11},{12,13},{... | collective-permute-start | bytes 27656 | tf_op jit(solution)/shard_map/ppermute | solution.py:28
  (21 other events, 415.4 us)
where the time goes:
time: 436 us; the launch traced here: 433 us
  starting transfers between devices  227 us (52%)
  waiting for transfers between devices  131 us (30%)
  local copies, waits for them, and re-layouts  47.8 us (11%)
  other arithmetic  16.7 us (4%)
  matrix products  8.67 us (2%)
    ppermute x40, starting transfers between devices, with_halo(): before = lax.ppermute(last, axis, up)  120 us
    ppermute x40, waiting for transfers between devices, with_halo(): before = lax.ppermute(last, axis, up)  95.6 us
    ppermute x40, starting transfers between devices, with_halo(): after = lax.ppermute(first, axis, down)  85.4 us
    all_to_all x1, waiting for transfers between devices, on_device(): lax.all_to_all(partials_out, 'space', split_axis=0, concat_axis=0, tiled=...  21.8 us
    all_to_all x1, waiting for transfers between devices, on_device(): lax.all_to_all(lax.all_to_all(partials_out, 'space', split_axis=0, concat...  12.6 us
    reshape x3, local copies, waits for them, and re-layouts, restrict(): field.reshape(sx // 2, 2, sy // 2, 2, sz // 2, 2).mean(axis=(1, 3, 5))  11 us
  transfers between devices with their start and end apart: 84, of which 40 were waited for; matrix products, arithmetic and copies ran while one was open for 9% of the time, Pallas kernels for 0%

commit v1 on v0

v1 whole, which is shorter than its diff:
```python
import functools
import math

import jax
import jax.numpy as jnp
from jax import lax
from jax.experimental import pallas as pl
from jax.experimental.pallas import tpu as pltpu
from jax.sharding import PartitionSpec as P

BRICK = 8
CX = 16
CY = 16
CZ = 128
LEVELS = 4
SWEEPS = 2
COARSE = 8


screen_weight = 0.05
relax_weight = 0.8


def splat_tiles(offsets_tile, samples_tile):
    tile_total = offsets_tile.shape[0]
    slot_total = offsets_tile.shape[2]
    centers = jnp.arange(BRICK, dtype=jnp.float32) + 0.5
    weights = jnp.maximum(
        0.0, 1.0 - jnp.abs(offsets_tile[:, :, None, :] - centers[None, None, :, None])
    )
    planar = (weights[:, 0, :, None, :] * weights[:, 1, None, :, :]).reshape(
        tile_total, BRICK * BRICK, slot_total
    )
    loaded = (samples_tile[:, :, None, :] * weights[:, 2][:, None, :, :]).reshape(
        tile_total, 4 * BRICK, slot_total
    )
    result = jnp.einsum("tas,tbs->tab", planar, loaded, precision=lax.Precision.HIGHEST)
    return result.reshape(tile_total, -1)


def splat_blocks(offsets_flat, samples_flat):
    tile_total = offsets_flat.shape[0]
    block_size = math.gcd(tile_total, 64)
    slot_total = offsets_flat.shape[2]

    def one_block(inputs):
        return splat_tiles(inputs[0], inputs[1])

    result = lax.map(
        one_block,
        (
            offsets_flat.reshape(tile_total // block_size, block_size, 3, slot_total),
            samples_flat.reshape(tile_total // block_size, block_size, 4, slot_total),
        ),
    )
    return result.reshape(tile_total, -1)


def to_grid(sums):
    shaped = sums.reshape(CX // BRICK, CY // BRICK, CZ // BRICK, BRICK, BRICK, 4, BRICK)
    return shaped.transpose(5, 0, 3, 1, 4, 2, 6).reshape(4, CX, CY, CZ)


HX = 4
HY = 8
MESH = pl.DeviceIdType.MESH
HIGHEST = lax.Precision.HIGHEST


def dot(a, b):
    return jnp.dot(a, b, precision=HIGHEST, preferred_element_type=jnp.float32)


def grid_iota(shape):
    return lax.broadcasted_iota(jnp.int32, shape, 0), lax.broadcasted_iota(jnp.int32, shape, 1)


def one_where(mask, value=1.0):
    return jnp.where(mask, jnp.float32(value), jnp.float32(0.0))


def shifted_z(c, zero_ends):
    zp = pltpu.roll(c, 127, c.ndim - 1)
    zm = pltpu.roll(c, 1, c.ndim - 1)
    if zero_ends:
        lane = lax.broadcasted_iota(jnp.int32, c.shape, c.ndim - 1)
        zp = jnp.where(lane < 127, zp, 0.0)
        zm = jnp.where(lane > 0, zm, 0.0)
    return zp + zm


def plane_neighbours(ref, x, zero_ends):
    c = ref[x]
    rows = c.shape[0]
    total = ref[x - 1] + ref[x + 1]
    total = total + pltpu.roll(c, 1, 0) + pltpu.roll(c, rows - 1, 0)
    return c, total + shifted_z(c, zero_ends)


def flat_neighbours(u, xs, zl, yl):
    row, lane = grid_iota(u.shape)
    rows = u.shape[0]
    xi, zi, yi = row % xs, lane % zl, lane // zl
    total = jnp.where(zi < zl - 1, pltpu.roll(u, 127, 1), 0.0)
    total = total + jnp.where(zi > 0, pltpu.roll(u, 1, 1), 0.0)
    total = total + jnp.where(xi < xs - 1, pltpu.roll(u, rows - 1, 0), 0.0)
    total = total + jnp.where(xi > 0, pltpu.roll(u, 1, 0), 0.0)
    far_up = pltpu.roll(pltpu.roll(u, zl * (yl - 1), 1), rows - xs, 0)
    far_up = jnp.where(row < rows - xs, far_up, 0.0)
    total = total + jnp.where(yi < yl - 1, pltpu.roll(u, 128 - zl, 1), far_up)
    far_down = pltpu.roll(pltpu.roll(u, 128 - zl * (yl - 1), 1), xs, 0)
    far_down = jnp.where(row >= xs, far_down, 0.0)
    return total + jnp.where(yi > 0, pltpu.roll(u, zl, 1), far_down)


class Halo:
    def __init__(self, ref, nx, ny, send, recv, base, has, place):
        self.ref, self.nx, self.ny = ref, nx, ny
        self.has = has
        self.items = []
        k = base
        for dx in (-1, 0, 1):
            for dy in (-1, 0, 1):
                if dx == 0 and dy == 0:
                    continue
                sx = {1: (nx, HX), -1: (HX, HX), 0: (HX, nx)}[dx]
                tx = {1: (0, HX), -1: (HX + nx, HX), 0: (HX, nx)}[dx]
                sy = {1: (ny, HY), -1: (HY, HY), 0: (HY, ny)}[dy]
                ty = {1: (0, HY), -1: (HY + ny, HY), 0: (HY, ny)}[dy]
                copy = pltpu.make_async_remote_copy(
                    src_ref=ref.at[pl.ds(*sx), pl.ds(*sy)],
                    dst_ref=ref.at[pl.ds(*tx), pl.ds(*ty)],
                    send_sem=send.at[k],
                    recv_sem=recv.at[k],
                    device_id=place(dx, dy),
                    device_id_type=MESH,
                )
                self.items.append((dx, dy, copy))
                k += 1

    def clear_rim(self):
        ref, nx, ny = self.ref, self.nx, self.ny

        @pl.when(jnp.logical_not(self.has(-1, 0)))
        def _():
            ref[0:HX] = jnp.zeros((HX,) + ref.shape[1:], jnp.float32)

        @pl.when(jnp.logical_not(self.has(1, 0)))
        def _():
            ref[HX + nx :] = jnp.zeros((HX,) + ref.shape[1:], jnp.float32)

        @pl.when(jnp.logical_not(self.has(0, -1)))
        def _():
            ref[:, 0:HY] = jnp.zeros((ref.shape[0], HY, 128), jnp.float32)

        @pl.when(jnp.logical_not(self.has(0, 1)))
        def _():
            ref[:, HY + ny :] = jnp.zeros((ref.shape[0], HY, 128), jnp.float32)

    def start(self):
        for dx, dy, copy in self.items:
            pl.when(self.has(dx, dy))(copy.start)

    def wait_recv(self):
        for dx, dy, copy in self.items:
            pl.when(self.has(-dx, -dy))(copy.wait_recv)

    def wait_send(self):
        for dx, dy, copy in self.items:
            pl.when(self.has(dx, dy))(copy.wait_send)


def planes(start, stop, unroll=2):
    def wrap(body):
        def step(x, carry):
            body(x)
            return carry

        lax.fori_loop(start, stop, step, 0, unroll=unroll)

    return wrap


def cycle_kernel(
    ns, nb, g, out,
    vxp, vyp, rhop, fp, ua, ub, wf, ws, rt,
    rho1p, f1p, u1a, u1b, wf1, ws1, rt1, pr,
    gsend, gath, f2g, rho2g, u2p, c2,
    send, recv, gsend_sem, grecv_sem,
):
    n = ns * nb
    sp, sb = lax.axis_index("space"), lax.axis_index("sub")
    me = sp * nb + sb

    def place(dx, dy):
        return (lax.rem(sp + dx + ns, ns), lax.rem(sb + dy + nb, nb))

    def has(dx, dy):
        ok = jnp.bool_(True)
        if dx:
            ok = sp + dx >= 0 if dx < 0 else sp + dx < ns
        if dy:
            oky = sb + dy >= 0 if dy < 0 else sb + dy < nb
            ok = jnp.logical_and(ok, oky) if dx else oky
        return ok

    barrier = pltpu.get_barrier_semaphore()

    def greet(k, carry):
        peer = lax.rem(me + k, n)
        pl.semaphore_signal(
            barrier, inc=1, device_id=(peer // nb, lax.rem(peer, nb)), device_id_type=MESH
        )
        return carry

    lax.fori_loop(1, n, greet, 0)

    rho_halo = Halo(rhop, 16, 16, send, recv, 0, has, place)
    f_halo = Halo(fp, 16, 16, send, recv, 8, has, place)
    rho1_halo = Halo(rho1p, 8, 8, send, recv, 16, has, place)
    f1_halo = Halo(f1p, 8, 8, send, recv, 24, has, place)

    def face(src, dst, k, dx, dy):
        return (
            dx,
            dy,
            pltpu.make_async_remote_copy(
                src_ref=src,
                dst_ref=dst,
                send_sem=send.at[k],
                recv_sem=recv.at[k],
                device_id=place(dx, dy),
                device_id_type=MESH,
            ),
        )

    faces = [
        face(vxp.at[16], vxp.at[0], 32, 1, 0),
        face(vxp.at[1], vxp.at[17], 33, -1, 0),
        face(vyp.at[:, pl.ds(16, 8)], vyp.at[:, pl.ds(0, 8)], 34, 0, 1),
        face(vyp.at[:, pl.ds(8, 8)], vyp.at[:, pl.ds(24, 8)], 35, 0, -1),
    ]
    vxp[1:17] = g[0]
    vyp[:, 8:24] = g[1]
    rhop[4:20, 8:24] = g[3]
    for halo in (rho_halo, f_halo, rho1_halo, f1_halo):
        halo.clear_rim()

    @pl.when(jnp.logical_not(has(-1, 0)))
    def _():
        vxp[0] = jnp.zeros((16, 128), jnp.float32)

    @pl.when(jnp.logical_not(has(1, 0)))
    def _():
        vxp[17] = jnp.zeros((16, 128), jnp.float32)

    @pl.when(jnp.logical_not(has(0, -1)))
    def _():
        vyp[:, 0:8] = jnp.zeros((16, 8, 128), jnp.float32)

    @pl.when(jnp.logical_not(has(0, 1)))
    def _():
        vyp[:, 24:32] = jnp.zeros((16, 8, 128), jnp.float32)

    zr, zc = grid_iota((128, 128))
    pool_z = one_where(zr // 2 == zc, 0.125)

    def pool_to_1(dst):
        pooled = rt[:, pl.ds(8, 8, stride=2), :] + rt[:, pl.ds(9, 8, stride=2), :]
        dst[4:12, 8:16] = dot(pooled.reshape(64, 128), pool_z).reshape(8, 8, 128)

    pool_lanes = one_where(zr // 2 == zc % 32, 0.125)
    prow = lax.broadcasted_iota(jnp.int32, (4, 8, 128), 1)
    plane_lane = lax.broadcasted_iota(jnp.int32, (4, 8, 128), 2)
    pick_rows = plane_lane // 32 == prow // 2

    def pool_to_2(value):
        spread = dot(value.reshape(32, 128), pool_lanes).reshape(4, 8, 128)
        return jnp.sum(jnp.where(pick_rows, spread, 0.0), axis=1)

    pl.semaphore_wait(barrier, n - 1)
    for dx, dy, copy in faces:
        pl.when(has(dx, dy))(copy.start)
    rho_halo.start()

    @planes(0, 8)
    def _(x):
        rt[x, 8:24] = g[3, 2 * x] + g[3, 2 * x + 1]

    pool_to_1(rho1p)
    rho1_halo.start()
    for i in range(4):
        rt1[i, 8:16] = rho1p[4 + 2 * i, 8:16] + rho1p[5 + 2 * i, 8:16]
    gsend[4:8] = pool_to_2(rt1[:, 8:16])

    for dx, dy, copy in faces:
        pl.when(has(-dx, -dy))(copy.wait_recv)

    lane16 = lax.broadcasted_iota(jnp.int32, (16, 128), 1)

    @planes(0, 16)
    def _(x):
        change = vxp[x + 2] - vxp[x]
        change = change + (vyp[x, 9:25] - vyp[x, 7:23])
        vz = g[2, x]
        zp = jnp.where(lane16 < 127, pltpu.roll(vz, 127, 1), 0.0)
        zm = jnp.where(lane16 > 0, pltpu.roll(vz, 1, 1), 0.0)
        fp[x + 4, 8:24] = -0.5 * (change + (zp - zm))

    f_halo.start()
    rho_halo.wait_recv()

    def inside(x, rows, lanes, step):
        r, l = grid_iota((rows, 128))
        gx = sp * step + x - HX
        gy = sb * step + r - HY
        ok = jnp.logical_and(gy >= 0, gy < nb * step)
        ok = jnp.logical_and(ok, jnp.logical_and(gx >= 0, gx < ns * step))
        return jnp.logical_and(ok, l < lanes) if lanes < 128 else ok

    @planes(0, 24)
    def _(x):
        ws[x] = jnp.where(inside(x, 32, 128, 16), relax_weight / (6.0 + screen_weight * rhop[x]), 0.0)

    rho1_halo.wait_recv()

    @planes(0, 16)
    def _(x):
        ws1[x] = jnp.where(
            inside(x, 24, 64, 8), relax_weight / (1.5 + screen_weight * rho1p[x]), 0.0
        )

    f_halo.wait_recv()

    @planes(1, 23)
    def _(x):
        value = ws[x] * fp[x]
        wf[x] = value
        ua[x] = value

    def sweeps(src, dst, wf_ref, ws_ref, scale, start, stop, zero_ends):
        @planes(start, stop)
        def _(x):
            c, total = plane_neighbours(src, x, zero_ends)
            if scale != 1.0:
                total = scale * total
            dst[x] = (1.0 - relax_weight) * c + (wf_ref[x] + ws_ref[x] * total)

    sweeps(ua, ub, wf, ws, 1.0, 2, 22, True)

    @planes(0, 8, 1)
    def _(x):
        parts = []
        for k in range(2):
            at = 4 + 2 * x + k
            c, total = plane_neighbours(ub, at, True)
            parts.append(fp[at] - (6.0 + screen_weight * rhop[at]) * c + total)
        rt[x] = parts[0] + parts[1]

    pool_to_1(f1p)
    f1_halo.start()
    f1_halo.wait_recv()

    @planes(0, 16)
    def _(x):
        value = ws1[x] * f1p[x]
        wf1[x] = value
        u1a[x] = value

    sweeps(u1a, u1b, wf1, ws1, 0.25, 1, 15, False)
    u1b[0] = jnp.zeros((24, 128), jnp.float32)
    u1b[15] = jnp.zeros((24, 128), jnp.float32)

    @planes(0, 4, 1)
    def _(x):
        parts = []
        for k in range(2):
            at = 4 + 2 * x + k
            c, total = plane_neighbours(u1b, at, False)
            parts.append(f1p[at] - (1.5 + screen_weight * rho1p[at]) * c + 0.25 * total)
        rt1[x] = parts[0] + parts[1]

    gsend[0:4] = pool_to_2(rt1[:, 8:16])
    mine = sb * ns + sp

    def tell(k, carry):
        peer = lax.rem(me + k, n)
        pltpu.make_async_remote_copy(
            src_ref=gsend,
            dst_ref=gath.at[mine],
            send_sem=gsend_sem,
            recv_sem=grecv_sem,
            device_id=(peer // nb, lax.rem(peer, nb)),
            device_id_type=MESH,
        ).start()
        return carry

    lax.fori_loop(1, n, tell, 0)
    gath[mine] = gsend[...]
    u2p[...] = jnp.zeros_like(u2p)
    every = gath.at[pl.ds(0, n - 1)]
    pltpu.make_async_copy(every, every, grecv_sem).wait()
    x2, x3 = ns * 4, ns * 2
    rows2, rows3 = nb * x2, nb * x3
    for b in range(nb):
        for s in range(ns):
            f2g[b, 4 * s : 4 * s + 4] = gath[b * ns + s, 0:4]
            rho2g[b, 4 * s : 4 * s + 4] = gath[b * ns + s, 4:8]
    f2 = f2g[...].reshape(rows2, 128)
    rho2 = rho2g[...].reshape(rows2, 128)
    diag2 = 0.375 + screen_weight * rho2
    w2 = relax_weight / diag2
    r3, r2 = grid_iota((rows3, rows2))
    pool_rows = one_where(r2 // 2 == r3)
    t2, t3 = grid_iota((rows2, rows3))
    grow_rows = one_where(t2 // 2 == t3)
    pool_l = one_where((zr // 64) * 16 + (zr % 32) // 2 == zc, 0.125)
    grow_l = one_where((zc // 64) * 16 + (zc % 32) // 2 == zr)
    rho3 = dot(dot(pool_rows, rho2), pool_l)
    lane3 = grid_iota((rows3, 128))[1]
    w3 = jnp.where(lane3 < 32, relax_weight / (0.09375 + screen_weight * rho3), 0.0)

    def step2(u):
        total = flat_neighbours(u, x2, 32, 4)
        return (1.0 - relax_weight) * u + w2 * (f2 + 0.0625 * total)

    u2 = step2(w2 * f2)
    res2 = f2 - diag2 * u2 + 0.0625 * flat_neighbours(u2, x2, 32, 4)
    f3 = dot(dot(pool_rows, res2), pool_l)
    u3 = w3 * f3
    for _ in range(COARSE - 1):
        total = flat_neighbours(u3, x3, 16, 2)
        u3 = (1.0 - relax_weight) * u3 + w3 * (f3 + 0.015625 * total)
    u2 = u2 + dot(grow_rows, dot(u3, grow_l))
    u2 = step2(step2(u2))
    u2p[1 : nb + 1, 8 : 8 + x2] = u2.reshape(nb, x2, 128)

    near = [u2p[sb + o, pl.ds(4 * sp + 6, 8), :] for o in range(3)]
    q0, q1 = grid_iota((128, 512))
    grow_q = one_where(
        jnp.logical_and(q0 // 32 == q1 // 128, jnp.logical_and(q0 % 32 == (q1 % 128) // 2, q1 % 128 < 64))
    )
    fan = dot(jnp.concatenate(near, axis=0), grow_q)
    order = [(0, 2), (0, 3), (1, 0), (1, 1), (1, 2), (1, 3), (2, 0), (2, 1)]
    for at, (o, j) in enumerate(order):
        c2[:, at, :] = fan[8 * o : 8 * o + 8, 128 * j : 128 * j + 128]
    for i in range(8):
        for k in range(2):
            for m in range(2):
                rows = pl.ds(4 + m, 8, stride=2)
                u1b[2 * i + k, rows, :] = u1b[2 * i + k, rows, :] + c2[i]
    sweeps(u1b, u1a, wf1, ws1, 0.25, 2, 14, False)
    sweeps(u1a, u1b, wf1, ws1, 0.25, 3, 13, False)
    grow_z = one_where(zr == zc // 2)
    pr[...] = dot(u1b[3:13].reshape(240, 128), grow_z).reshape(10, 24, 128)

    @planes(0, 10, 1)
    def _(i):
        for k in range(2):
            for m in range(2):
                rows = pl.ds(m, 16, stride=2)
                ub[2 * i + 2 + k, rows, :] = ub[2 * i + 2 + k, rows, :] + pr[i, 4:20]

    sweeps(ub, ua, wf, ws, 1.0, 3, 21, True)

    @planes(4, 20)
    def _(x):
        c, total = plane_neighbours(ua, x, True)
        full = (1.0 - relax_weight) * c + (wf[x] + ws[x] * total)
        out[x - 4] = full[8:24]

    for halo in (rho_halo, f_halo, rho1_halo, f1_halo):
        halo.wait_send()
    for dx, dy, copy in faces:
        pl.when(has(dx, dy))(copy.wait_send)
    pltpu.make_async_copy(every, every, gsend_sem).wait()


def cycle(grid):
    ns, nb = lax.axis_size("space"), lax.axis_size("sub")
    n = ns * nb
    vm = lambda *shape: pltpu.VMEM(shape, jnp.float32)
    fine, mid = (24, 32, 128), (16, 24, 128)
    return pl.pallas_call(
        functools.partial(cycle_kernel, ns, nb),
        out_shape=jax.ShapeDtypeStruct((CX, CY, CZ), jnp.float32),
        in_specs=[pl.BlockSpec(memory_space=pltpu.VMEM)],
        out_specs=pl.BlockSpec(memory_space=pltpu.VMEM),
        scratch_shapes=[
            vm(18, 16, 128), vm(16, 32, 128), vm(*fine), vm(*fine), vm(*fine), vm(*fine),
            vm(*fine), vm(*fine), vm(8, 32, 128),
            vm(*mid), vm(*mid), vm(*mid), vm(*mid), vm(*mid), vm(*mid), vm(4, 24, 128),
            vm(10, 24, 128),
            vm(8, 128), vm(n, 8, 128), vm(nb, ns * 4, 128), vm(nb, ns * 4, 128),
            vm(nb + 2, ns * 4 + 16, 128), vm(8, 8, 128),
            pltpu.SemaphoreType.DMA((36,)),
            pltpu.SemaphoreType.DMA((36,)),
            pltpu.SemaphoreType.DMA,
            pltpu.SemaphoreType.DMA,
        ],
        compiler_params=pltpu.CompilerParams(
            collective_id=0, has_side_effects=True, vmem_limit_bytes=48 * 1024 * 1024
        ),
        name="cycle",
    )(grid)


def on_device(offsets, normals, density, tile_brick, tile_count):
    space_count = lax.axis_size("space")
    sub_count = lax.axis_size("sub")
    tiles_each = offsets.shape[4]
    slot_total = offsets.shape[6]
    brick_total = CX // BRICK * (CY // BRICK) * (CZ // BRICK)
    offsets_local = offsets.reshape(space_count, sub_count, tiles_each, 3, slot_total)
    samples = jnp.concatenate(
        [
            normals.reshape(space_count, sub_count, tiles_each, 3, slot_total),
            density.reshape(space_count, sub_count, tiles_each, 1, slot_total),
        ],
        axis=3,
    )
    slot_numbers = lax.broadcasted_iota(
        jnp.int32, (space_count, sub_count, tiles_each, slot_total), 3
    )
    live_slots = (
        slot_numbers < tile_count.reshape(space_count, sub_count, tiles_each)[..., None]
    ).astype(jnp.float32)
    samples = samples * live_slots[:, :, :, None, :]
    brick_ids = tile_brick.reshape(space_count, sub_count, tiles_each).astype(jnp.float32)
    partials_out = splat_blocks(
        offsets_local.reshape(-1, 3, slot_total), samples.reshape(-1, 4, slot_total)
    )
    partials_out = partials_out.reshape(space_count, sub_count, tiles_each, -1)
    partials_in, brick_in = (
        lax.all_to_all(
            lax.all_to_all(partials_out, "space", split_axis=0, concat_axis=0, tiled=True),
            "sub",
            split_axis=1,
            concat_axis=1,
            tiled=True,
        ),
        lax.all_to_all(
            lax.all_to_all(brick_ids, "space", split_axis=0, concat_axis=0, tiled=True),
            "sub",
            split_axis=1,
            concat_axis=1,
            tiled=True,
        ),
    )
    partials = partials_in.reshape(space_count * sub_count * tiles_each, -1)
    brick_numbers = jnp.arange(brick_total, dtype=jnp.float32)
    onehot = (brick_in.reshape(-1)[None, :] == brick_numbers[:, None]).astype(jnp.float32)
    sums = jnp.dot(
        onehot, partials, precision=lax.Precision.HIGHEST, preferred_element_type=jnp.float32
    )
    grid = to_grid(sums)
    density_field = grid[3]
    indicator = cycle(grid)
    return (indicator, density_field)


def solution(mesh):
    placed = (
        P("space", "sub", None, None, None, None, None),
        P("space", "sub", None, None, None, None, None),
        P("space", "sub", None, None, None, None),
        P("space", "sub", None, None, None),
        P("space", "sub", None, None, None),
    )
    return jax.shard_map(
        on_device,
        mesh=mesh,
        in_specs=placed,
        out_specs=(P("space", "sub", None), P("space", "sub", None)),
        check_vma=False,
    )
```

time: 436 us -> 135 us (0.31)
  the two profiles are of different devices: /device:TPU:28 before, /device:TPU:0 now
where the time goes in v1:
time: 135 us; the launch traced here: 134 us
  waiting for transfers between devices  41.7 us (31%)
  local copies, waits for them, and re-layouts  31.8 us (24%)
  Pallas kernels  28.9 us (21%)
  starting transfers between devices  20 us (15%)
  matrix products  8.74 us (6%)
  other arithmetic  2.2 us (2%)
    pallas_call x1, Pallas kernels, cycle(): pl.pallas_call(functools.partial(cycle_kernel, ns, nb), out_shape=jax.Sha...  28.9 us
    all_to_all x1, waiting for transfers between devices, on_device(): lax.all_to_all(partials_out, 'space', split_axis=0, concat_axis=0, tiled=...  24.7 us
    all_to_all x1, waiting for transfers between devices, on_device(): lax.all_to_all(lax.all_to_all(partials_out, 'space', split_axis=0, concat...  14.2 us
    all_to_all x1, starting transfers between devices, on_device(): lax.all_to_all(brick_ids, 'space', split_axis=0, concat_axis=0, tiled=True)  7.25 us
    transpose x1, local copies, waits for them, and re-layouts, to_grid(): return shaped.transpose(5, 0, 3, 1, 4, 2, 6).reshape(4, CX, CY, CZ)  7.06 us
    dot_general x2, matrix products, splat_tiles(): jnp.einsum('tas,tbs->tab', planar, loaded, precision=lax.Precision.HIGHEST)  6.77 us
    reshape x1, local copies, waits for them, and re-layouts, to_grid(): return shaped.transpose(5, 0, 3, 1, 4, 2, 6).reshape(4, CX, CY, CZ)  6.37 us
    all_to_all x1, starting transfers between devices, on_device(): lax.all_to_all(partials_out, 'space', split_axis=0, concat_axis=0, tiled=...  6 us
  transfers between devices with their start and end apart: 4, of which 3 were waited for; matrix products, arithmetic and copies ran while one was open for 15% of the time, Pallas kernels for 0%

profile of v1, /device:TPU:0, one launch (start us, length us, event | category | flops | bytes accessed | tf_op | source)
XLA Modules:
  0.0 134.2 jit_solution(3372079659588881745)
XLA Ops:
  0.6 0.7 convert_bitcast_fusion
  1.3 0.7 copy.44
  2.0 7.3 %all-to-all-start = ((f32[8,4,4]{2,1,0:T(4,128)}), f32[8,4,4]{2,1,0:T(4,128)S(1)}, u32[]{:S(2)}, u32[]{:S(2)}) async-start(f32[8,4,4]{2,1,0:T(4,128)} %copy.44), calls=%async_computation | async-start | bytes 32768 | tf_op jit(solution)/shard_map/all_to_all | solution.py:543
  9.3 0.8 copy.49
  10.1 0.1 lt.17
  10.2 0.1 fusion.9
  10.3 1.0 copy.47
  11.2 1.0 copy.48
  12.2 1.0 maximum_multiply_fusion
  13.2 11.9 %while.10 = (s32[]{:T(128)}, f32[2,64,2048]{2,1,0:T(8,128)}, f32[2,64,3,128]{3,1,0,2:T(8,128)S(1)}, f32[2,64,4,128]{3,2,1,0:T(4,128)S(1)}, s32[]{:T(128)}) while((s32[]{:T(128)}, f32[2,64,2048]{2,1,0:T(8,128)}, f32[2,64,3,128]{3,1,0,2:T(8,128)S(1)}, f32[2,64,4,128]{3,2,1,0:T(4,128)S(1)}, s32[]{:T(128)}) %tuple.35), condition=%wide.region_1.2_spmd, body=%wide.region_0.1_spmd.sunk | while | flops 202899472 | bytes 7504017 | solution.py:49
  13.3 0.2 subtract_maximum_fusion.2
  13.5 0.1 slice_bitcast_fusion.4
  13.6 3.4 %fusion.20 = f32[64,64,32]{1,2,0:T(8,128)S(1)} fusion(f32[64,8,128]{2,1,0:T(8,128)S(1)} %get-tuple-element.80, f32[64,8,128]{2,1,0:T(8,128)S(1)} %get-tuple-element.81, f32[64,8,128]{2,1,0:T(8,128)S(1)} %get-tuple-element.82, f32[64,4,128]{2,1,0:T(4,128)S(1)} %dynamic-slice_bitcast_fusion.5), kind=kOutput, calls=%fused_computation.clone.1 | convolution fusion | flops 202113024 | bytes 1441792 | tf_op jit(solution)/shard_map/while/body/eval_jaxpr/tas,tbs->tab/dot_general | solution.py:37
  17.0 1.1 copy.64
  18.1 0.3 copy.65
  18.4 0.8 constant_dynamic-update-slice_fusion.2
  19.3 0.2 subtract_maximum_fusion.2
  19.5 0.1 slice_bitcast_fusion.4
  19.5 3.4 %fusion.20 = f32[64,64,32]{1,2,0:T(8,128)S(1)} fusion(f32[64,8,128]{2,1,0:T(8,128)S(1)} %get-tuple-element.80, f32[64,8,128]{2,1,0:T(8,128)S(1)} %get-tuple-element.81, f32[64,8,128]{2,1,0:T(8,128)S(1)} %get-tuple-element.82, f32[64,4,128]{2,1,0:T(4,128)S(1)} %dynamic-slice_bitcast_fusion.5), kind=kOutput, calls=%fused_computation.clone.1 | convolution fusion | flops 202113024 | bytes 1441792 | tf_op jit(solution)/shard_map/while/body/eval_jaxpr/tas,tbs->tab/dot_general | solution.py:37
  22.9 1.1 copy.64
  24.0 0.3 copy.65
  24.3 0.8 constant_dynamic-update-slice_fusion.2
  25.2 2.5 %reshape_reshape.4 = f32[8,4,4,2048]{3,2,1,0:T(4,128)} reshape(f32[2,64,2048]{2,1,0:T(8,128)} %get-tuple-element.24) | data formatting | bytes 2097152 | tf_op jit(solution)/shard_map/reshape;reshape | solution.py:533
  27.7 0.0 all-to-all-done
  27.7 6.0 %all-to-all-start.2 = ((f32[8,4,4,2048]{3,2,1,0:T(4,128)}), f32[8,4,4,2048]{3,2,1,0:T(4,128)S(1)}, u32[]{:S(2)}, u32[]{:S(2)}) async-start(f32[8,4,4,2048]{3,2,1,0:T(4,128)} %reshape_reshape.4), calls=%async_computation.2 | async-start | bytes 2097152 | tf_op jit(solution)/shard_map/all_to_all | solution.py:536
  33.7 0.7 copy.45
  34.4 24.7 %all-to-all-done.2 = f32[8,4,4,2048]{3,2,1,0:T(4,128)S(1)} async-done(((f32[8,4,4,2048]{3,2,1,0:T(4,128)}), f32[8,4,4,2048]{3,2,1,0:T(4,128)S(1)}, u32[]{:S(2)}, u32[]{:S(2)}) %all-to-all-start.2) | async-done | bytes 1048608 | tf_op jit(solution)/shard_map/all_to_all | solution.py:536
  59.1 3.2 %all-to-all-start.1 = ((f32[8,4,4]{0,2,1:T(4,128)}), f32[8,4,4]{0,2,1:T(4,128)S(1)}, u32[]{:S(2)}, u32[]{:S(2)}) async-start(f32[8,4,4]{0,2,1:T(4,128)} %copy.45), calls=%async_computation.1 | async-start | bytes 16384 | tf_op jit(solution)/shard_map/all_to_all | solution.py:542
  62.4 1.0 copy.52
  63.5 2.7 %all-to-all-done.1 = f32[8,4,4]{0,2,1:T(4,128)S(1)} async-done(((f32[8,4,4]{0,2,1:T(4,128)}), f32[8,4,4]{0,2,1:T(4,128)S(1)}, u32[]{:S(2)}, u32[]{:S(2)}) %all-to-all-start.1) | async-done | bytes 544 | tf_op jit(solution)/shard_map/all_to_all | solution.py:542
  66.2 3.5 %all-to-all-start.3 = ((f32[8,4,4,2048]{3,2,0,1:T(4,128)}), f32[8,4,4,2048]{3,2,0,1:T(4,128)S(1)}, u32[]{:S(2)}, u32[]{:S(2)}) async-start(f32[8,4,4,2048]{3,2,0,1:T(4,128)} %copy.52), calls=%async_computation.3 | async-start | bytes 2097152 | tf_op jit(solution)/shard_map/all_to_all | solution.py:535
  69.7 0.1 copy.46
  69.8 0.1 eq.32
  69.9 14.2 %all-to-all-done.3 = f32[8,4,4,2048]{3,2,0,1:T(4,128)S(1)} async-done(((f32[8,4,4,2048]{3,2,0,1:T(4,128)}), f32[8,4,4,2048]{3,2,0,1:T(4,128)S(1)}, u32[]{:S(2)}, u32[]{:S(2)}) %all-to-all-start.3) | async-done | bytes 1048608 | tf_op jit(solution)/shard_map/all_to_all | solution.py:535
  84.1 0.1 copy.53
  84.2 0.4 reshape.74
  84.6 0.3 copy.54
  84.9 2.0 %convolution_bitcast_fusion = f32[4,2,8,2,8,16,8]{5,6,0,4,2,3,1:T(8,128)S(1)} fusion(f32[8,8,4,8,128,1,1]{4,3,2,1,0,6,5:T(8,128)S(1)} %bitcast.56, f32[2,2,16]{2,1,0:T(2,128)S(1)} %multiply_add_fusion, f32[128]{0:T(128)S(1)} %eq.32), kind=kOutput, calls=%fused_computation.17 | convolution fusion | flops 201334784 | bytes 1573632 | tf_op jit(solution)/shard_map/dot_general | solution.py:553
  86.9 0.0 copy-start
  86.9 1.9 %copy-done = f32[4,2,8,2,8,16,8]{5,6,0,4,2,3,1:T(8,128)} copy-done((f32[4,2,8,2,8,16,8]{5,6,0,4,2,3,1:T(8,128)}, f32[4,2,8,2,8,16,8]{5,6,0,4,2,3,1:T(8,128)S(1)}, u32[]{:S(2)}) %copy-start) | copy-done | bytes 524312
  88.9 0.0 slice-start
  88.9 7.1 %copy.55 = f32[4,2,8,2,8,16,8]{6,5,4,3,2,1,0:T(8,128)} copy(f32[4,2,8,2,8,16,8]{5,6,0,4,2,3,1:T(8,128)} %copy-done) | data formatting | bytes 1048576 | tf_op jit(solution)/shard_map/transpose | solution.py:61
  95.9 0.0 slice-done
  95.9 0.6 copy.56
  96.6 1.6 %squeeze.8 = f32[16,16,128]{2,1,0:T(8,128)} reshape(f32[1,2,8,2,8,16,8]{6,5,4,3,2,1,0:T(8,128)S(1)} %copy.56) | data formatting | bytes 262144 | tf_op jit(solution)/shard_map/squeeze | solution.py:557
  98.2 6.4 %reshape.75.g = f32[4,16,16,128]{3,2,1,0:T(8,128)S(1)} reshape(f32[4,2,8,2,8,16,8]{6,5,4,3,2,1,0:T(8,128)} %copy.55) | data formatting | bytes 1048576 | tf_op jit(solution)/shard_map/reshape | solution.py:61
  104.6 28.9 %cycle.1 = f32[16,16,128]{2,1,0:T(8,128)S(1)} custom-call(f32[4,16,16,128]{3,2,1,0:T(8,128)S(1)} %reshape.75.g), custom_call_target="tpu_custom_call" | custom-call | tf_op jit(solution)/shard_map/cycle/pallas_call | solution.py:484
  133.5 0.7 copy.76
  (8 shorter events, 0.1 us)
Async XLA Ops:
  2.0 25.7 %all-to-all-start = ((f32[8,4,4]{2,1,0:T(4,128)}), f32[8,4,4]{2,1,0:T(4,128)S(1)}, u32[]{:S(2)}, u32[]{:S(2)}) async-start(f32[8,4,4]{2,1,0:T(4,128)} %copy.44), calls=%async_computation | async-start | bytes 32768 | tf_op jit(solution)/shard_map/all_to_all | solution.py:543
  27.7 31.4 %all-to-all-start.2 = ((f32[8,4,4,2048]{3,2,1,0:T(4,128)}), f32[8,4,4,2048]{3,2,1,0:T(4,128)S(1)}, u32[]{:S(2)}, u32[]{:S(2)}) async-start(f32[8,4,4,2048]{3,2,1,0:T(4,128)} %reshape_reshape.4), calls=%async_computation.2 | async-start | bytes 2097152 | tf_op jit(solution)/shard_map/all_to_all | solution.py:536
  59.1 7.0 %all-to-all-start.1 = ((f32[8,4,4]{0,2,1:T(4,128)}), f32[8,4,4]{0,2,1:T(4,128)S(1)}, u32[]{:S(2)}, u32[]{:S(2)}) async-start(f32[8,4,4]{0,2,1:T(4,128)} %copy.45), calls=%async_computation.1 | async-start | bytes 16384 | tf_op jit(solution)/shard_map/all_to_all | solution.py:542
  66.2 18.0 %all-to-all-start.3 = ((f32[8,4,4,2048]{3,2,0,1:T(4,128)}), f32[8,4,4,2048]{3,2,0,1:T(4,128)S(1)}, u32[]{:S(2)}, u32[]{:S(2)}) async-start(f32[8,4,4,2048]{3,2,0,1:T(4,128)} %copy.52), calls=%async_computation.3 | async-start | bytes 2097152 | tf_op jit(solution)/shard_map/all_to_all | solution.py:535
  86.9 2.0 %copy-start = (f32[4,2,8,2,8,16,8]{5,6,0,4,2,3,1:T(8,128)}, f32[4,2,8,2,8,16,8]{5,6,0,4,2,3,1:T(8,128)S(1)}, u32[]{:S(2)}) copy-start(f32[4,2,8,2,8,16,8]{5,6,0,4,2,3,1:T(8,128)S(1)} %convolution_bitcast_fusion) | copy-start | bytes 1572868
  88.9 7.1 %slice-start = ((f32[4,2,8,2,8,16,8]{5,6,0,4,2,3,1:T(8,128)}), f32[1,2,8,2,8,16,8]{5,6,0,4,2,3,1:T(8,128)S(1)}, s32[]{:S(2)}) async-start(f32[4,2,8,2,8,16,8]{5,6,0,4,2,3,1:T(8,128)} %copy-done), calls=%async_computation.4 | async-start | bytes 2097152 | tf_op jit(solution)/shard_map/slice | solution.py:557

commit v2 on v1

--- a/solution.py
+++ b/solution.py
@@ -1,5 +1,4 @@
 import functools
-import math
 
 import jax
 import jax.numpy as jnp
@@ -19,46 +18,6 @@
 
 screen_weight = 0.05
 relax_weight = 0.8
-
-
-def splat_tiles(offsets_tile, samples_tile):
-    tile_total = offsets_tile.shape[0]
-    slot_total = offsets_tile.shape[2]
-    centers = jnp.arange(BRICK, dtype=jnp.float32) + 0.5
-    weights = jnp.maximum(
-        0.0, 1.0 - jnp.abs(offsets_tile[:, :, None, :] - centers[None, None, :, None])
-    )
-    planar = (weights[:, 0, :, None, :] * weights[:, 1, None, :, :]).reshape(
-        tile_total, BRICK * BRICK, slot_total
-    )
-    loaded = (samples_tile[:, :, None, :] * weights[:, 2][:, None, :, :]).reshape(
-        tile_total, 4 * BRICK, slot_total
-    )
-    result = jnp.einsum("tas,tbs->tab", planar, loaded, precision=lax.Precision.HIGHEST)
-    return result.reshape(tile_total, -1)
-
-
-def splat_blocks(offsets_flat, samples_flat):
-    tile_total = offsets_flat.shape[0]
-    block_size = math.gcd(tile_total, 64)
-    slot_total = offsets_flat.shape[2]
-
-    def one_block(inputs):
-        return splat_tiles(inputs[0], inputs[1])
-
-    result = lax.map(
-        one_block,
-        (
-            offsets_flat.reshape(tile_total // block_size, block_size, 3, slot_total),
-            samples_flat.reshape(tile_total // block_size, block_size, 4, slot_total),
-        ),
-    )
-    return result.reshape(tile_total, -1)
-
-
-def to_grid(sums):
-    shaped = sums.reshape(CX // BRICK, CY // BRICK, CZ // BRICK, BRICK, BRICK, 4, BRICK)
-    return shaped.transpose(5, 0, 3, 1, 4, 2, 6).reshape(4, CX, CY, CZ)
 
 
 HX = 4
@@ -505,58 +464,152 @@
     )(grid)
 
 
+def exchange_kernel(ns, nb, src, dst, send_sem, recv_sem, own_sem):
+    n = ns * nb
+    me = lax.axis_index("space") * nb + lax.axis_index("sub")
+    barrier = pltpu.get_barrier_semaphore()
+
+    def where(k):
+        peer = lax.rem(me + k, n)
+        return peer, (peer // nb, lax.rem(peer, nb))
+
+    def greet(k, carry):
+        pl.semaphore_signal(barrier, inc=1, device_id=where(k)[1], device_id_type=MESH)
+        return carry
+
+    lax.fori_loop(1, n, greet, 0)
+    own = pltpu.make_async_copy(src.at[me], dst.at[me], own_sem)
+    own.start()
+    pl.semaphore_wait(barrier, n - 1)
+
+    def tell(k, carry):
+        peer, place = where(k)
+        pltpu.make_async_remote_copy(
+            src_ref=src.at[peer],
+            dst_ref=dst.at[me],
+            send_sem=send_sem,
+            recv_sem=recv_sem,
+            device_id=place,
+            device_id_type=MESH,
+        ).start()
+        return carry
+
+    lax.fori_loop(1, n, tell, 0)
+    own.wait()
+    every = dst.at[pl.ds(0, n - 1)]
+    pltpu.make_async_copy(every, every, recv_sem).wait()
+    pltpu.make_async_copy(every, every, send_sem).wait()
+
+
+def exchange(packed):
+    ns, nb = lax.axis_size("space"), lax.axis_size("sub")
+    return pl.pallas_call(
+        functools.partial(exchange_kernel, ns, nb),
+        out_shape=jax.ShapeDtypeStruct(packed.shape, jnp.float32),
+        in_specs=[pl.BlockSpec(memory_space=pl.ANY)],
+        out_specs=pl.BlockSpec(memory_space=pl.ANY),
+        scratch_shapes=[pltpu.SemaphoreType.DMA] * 3,
+        compiler_params=pltpu.CompilerParams(collective_id=1, has_side_effects=True),
+        name="exchange",
+    )(packed)
+
+
+def splat_kernel(ids, points, grid, acc):
+    peers, tiles = points.shape[0], points.shape[1]
+    acc[...] = jnp.zeros_like(acc)
+    centers = lax.broadcasted_iota(jnp.int32, (BRICK, 128), 0).astype(jnp.float32) + 0.5
+
+    def split(value):
+        high = value.astype(jnp.bfloat16)
+        low = (value - high.astype(jnp.float32)).astype(jnp.bfloat16)
+        return jnp.concatenate([high, low], axis=0)
+
+    def one_tile(p, t):
+        rows = points[p, t]
+        wx, wy, wz = (
+            jnp.maximum(0.0, 1.0 - jnp.abs(rows[d : d + 1] - centers)) for d in range(3)
+        )
+        planar = jnp.concatenate([wx[i : i + 1] * wy for i in range(BRICK)], axis=0)
+        loaded = jnp.concatenate([rows[3 + c : 4 + c] * wz for c in range(4)], axis=0)
+        full = lax.dot_general(
+            split(planar),
+            split(loaded),
+            (((1,), (1,)), ((), ())),
+            preferred_element_type=jnp.float32,
+        )
+        return full[0:64] + full[64:128]
+
+    def one_peer(p, carry):
+        parts = [one_tile(p, t) for t in range(tiles)]
+        for t in range(tiles):
+            brick = ids[p * tiles + t]
+            acc[brick, :, 0:64] = acc[brick, :, 0:64] + parts[t]
+        return carry
+
+    lax.fori_loop(0, peers, one_peer, 0, unroll=2)
+
+    group = lax.broadcasted_iota(jnp.int32, (BRICK, 128), 1) // BRICK
+    nz = CZ // BRICK
+
+    for column in range(acc.shape[0] // nz):
+        bx, by = column // (CY // BRICK), column % (CY // BRICK)
+
+        def one_row(i, carry):
+            turned = []
+            for bz in range(nz):
+                part = acc[column * nz + bz, pl.ds(pl.multiple_of(8 * i, 8), 8), :]
+                part = part + pltpu.roll(part, 96, 1)
+                turned.append(pltpu.roll(part, 8 * bz, 1) if bz else part)
+            for c in range(4):
+                value = turned[0]
+                for bz in range(1, nz):
+                    value = jnp.where(group == (bz + c) % nz, turned[bz], value)
+                if c:
+                    value = pltpu.roll(value, 128 - 8 * c, 1)
+                grid[c, BRICK * bx + i, BRICK * by : BRICK * by + BRICK, :] = value
+            return carry
+
+        lax.fori_loop(0, BRICK, one_row, 0, unroll=2)
+
+
+def splat(ids, points):
+    bricks = CX // BRICK * (CY // BRICK) * (CZ // BRICK)
+    return pl.pallas_call(
+        splat_kernel,
+        out_shape=jax.ShapeDtypeStruct((4, CX, CY, CZ), jnp.float32),
+        in_specs=[
+            pl.BlockSpec(memory_space=pltpu.SMEM),
+            pl.BlockSpec(memory_space=pltpu.VMEM),
+        ],
+        out_specs=pl.BlockSpec(memory_space=pltpu.VMEM),
+        scratch_shapes=[pltpu.VMEM((bricks, 64, 128), jnp.float32)],
+        compiler_params=pltpu.CompilerParams(vmem_limit_bytes=48 * 1024 * 1024),
+        name="splat",
+    )(ids, points)
+
+
 def on_device(offsets, normals, density, tile_brick, tile_count):
-    space_count = lax.axis_size("space")
-    sub_count = lax.axis_size("sub")
-    tiles_each = offsets.shape[4]
-    slot_total = offsets.shape[6]
-    brick_total = CX // BRICK * (CY // BRICK) * (CZ // BRICK)
-    offsets_local = offsets.reshape(space_count, sub_count, tiles_each, 3, slot_total)
-    samples = jnp.concatenate(
+    devices = lax.axis_size("space") * lax.axis_size("sub")
+    tiles, slots = offsets.shape[4], offsets.shape[6]
+    live = lax.broadcasted_iota(jnp.int32, (devices, tiles, 1, slots), 3) < tile_count.reshape(
+        devices, tiles, 1, 1
+    )
+    ids = jnp.broadcast_to(
+        tile_brick.reshape(devices, tiles, 1, 1).astype(jnp.float32), (devices, tiles, 1, slots)
+    )
+    packed = jnp.concatenate(
         [
-            normals.reshape(space_count, sub_count, tiles_each, 3, slot_total),
-            density.reshape(space_count, sub_count, tiles_each, 1, slot_total),
+            offsets.reshape(devices, tiles, 3, slots),
+            jnp.where(live, normals.reshape(devices, tiles, 3, slots), 0.0),
+            jnp.where(live, density.reshape(devices, tiles, 1, slots), 0.0),
+            ids,
         ],
-        axis=3,
+        axis=2,
     )
-    slot_numbers = lax.broadcasted_iota(
-        jnp.int32, (space_count, sub_count, tiles_each, slot_total), 3
-    )
-    live_slots = (
-        slot_numbers < tile_count.reshape(space_count, sub_count, tiles_each)[..., None]
-    ).astype(jnp.float32)
-    samples = samples * live_slots[:, :, :, None, :]
-    brick_ids = tile_brick.reshape(space_count, sub_count, tiles_each).astype(jnp.float32)
-    partials_out = splat_blocks(
-        offsets_local.reshape(-1, 3, slot_total), samples.reshape(-1, 4, slot_total)
-    )
-    partials_out = partials_out.reshape(space_count, sub_count, tiles_each, -1)
-    partials_in, brick_in = (
-        lax.all_to_all(
-            lax.all_to_all(partials_out, "space", split_axis=0, concat_axis=0, tiled=True),
-            "sub",
-            split_axis=1,
-            concat_axis=1,
-            tiled=True,
-        ),
-        lax.all_to_all(
-            lax.all_to_all(brick_ids, "space", split_axis=0, concat_axis=0, tiled=True),
-            "sub",
-            split_axis=1,
-            concat_axis=1,
-            tiled=True,
-        ),
-    )
-    partials = partials_in.reshape(space_count * sub_count * tiles_each, -1)
-    brick_numbers = jnp.arange(brick_total, dtype=jnp.float32)
-    onehot = (brick_in.reshape(-1)[None, :] == brick_numbers[:, None]).astype(jnp.float32)
-    sums = jnp.dot(
-        onehot, partials, precision=lax.Precision.HIGHEST, preferred_element_type=jnp.float32
-    )
-    grid = to_grid(sums)
-    density_field = grid[3]
-    indicator = cycle(grid)
-    return (indicator, density_field)
+    points = exchange(packed)
+    bricks = points[:, :, 7, 0].astype(jnp.int32).reshape(-1)
+    grid = splat(bricks, points)
+    return (cycle(grid), grid[3])
 
 
 def solution(mesh):

time: 135 us -> 69 us (0.51)
  waiting for transfers between devices: 41.7 us -> 0 us
  Pallas kernels: 28.9 us -> 57.9 us
  local copies, waits for them, and re-layouts: 31.8 us -> 4.56 us
  starting transfers between devices: 20 us -> 0 us
  matrix products: 8.74 us -> 0 us
  other arithmetic: 2.2 us -> 5.57 us
    all_to_all x4 -> x0, waiting for transfers between devices: 41.7 us -> none  [the longest x1 24.7 us: on_device(): lax.all_to_all(partials_out, 'space', split_axis=0, concat_axis=0, tiled=...]
    pallas_call x0 -> x2, Pallas kernels: none -> 24.4 us  [the longest x1 16.2 us: exchange(): pl.pallas_call(functools.partial(exchange_kernel, ns, nb), out_shape=jax....]
    all_to_all x4 -> x0, starting transfers between devices: 20 us -> none  [the longest x1 7.25 us: on_device(): lax.all_to_all(brick_ids, 'space', split_axis=0, concat_axis=0, tiled=True)]
    dot_general x3 -> x0, matrix products: 8.74 us -> none  [the longest x2 6.77 us: splat_tiles(): jnp.einsum('tas,tbs->tab', planar, loaded, precision=lax.Precision.HIGHEST)]
    transpose x1 -> x0, local copies, waits for them, and re-layouts: 7.06 us -> none  [to_grid(): return shaped.transpose(5, 0, 3, 1, 4, 2, 6).reshape(4, CX, CY, CZ)]
    reshape x2 -> x0, local copies, waits for them, and re-layouts: 6.74 us -> none  [the longest x1 6.37 us: to_grid(): return shaped.transpose(5, 0, 3, 1, 4, 2, 6).reshape(4, CX, CY, CZ)]
    pallas_call x1, Pallas kernels: 28.9 us -> 33.4 us  [cycle(): pl.pallas_call(functools.partial(cycle_kernel, ns, nb), out_shape=jax.Sha...]
    convert_element_type x2, other arithmetic: 0.79 us -> 4.13 us  [the longest x1 3.39 us: on_device(): bricks = points[:, :, 7, 0].astype(jnp.int32).reshape(-1)]
  transfers between devices with their start and end apart: 4 -> 0, of which waited for: 3 -> 0; matrix products, arithmetic and copies ran while one was open for 15% -> 0% of each run, Pallas kernels for 0% -> 0%
where the time goes in v2:
time: 69 us; the launch traced here: 68.7 us
  Pallas kernels  57.9 us (84%)
  other arithmetic  5.57 us (8%)
  local copies, waits for them, and re-layouts  4.56 us (7%)
  between operations  0.74 us (1%)
    pallas_call x1, Pallas kernels, cycle(): pl.pallas_call(functools.partial(cycle_kernel, ns, nb), out_shape=jax.Sha...  33.4 us
    pallas_call x1, Pallas kernels, exchange(): pl.pallas_call(functools.partial(exchange_kernel, ns, nb), out_shape=jax....  16.2 us
    pallas_call x1, Pallas kernels, splat(): pl.pallas_call(splat_kernel, out_shape=jax.ShapeDtypeStruct((4, CX, CY, C...  8.25 us
    convert_element_type x1, other arithmetic, on_device(): bricks = points[:, :, 7, 0].astype(jnp.int32).reshape(-1)  3.39 us
    unnamed x11, local copies, waits for them, and re-layouts  2.69 us

profile of v2, /device:TPU:0, one launch (start us, length us, event | category | flops | bytes accessed | tf_op | source)
XLA Modules:
  0.0 68.7 jit_solution(5499828710562553058)
XLA Ops:
  0.6 0.0 copy-start.3
  0.6 0.0 copy-start.1
  0.6 0.7 %convert_element_type.18 = f32[1,1,8,4,4]{2,4,3,1,0:T(4,128)S(1)} convert(s32[1,1,8,4,4]{2,4,3,1,0:T(4,128)} %param.8) | non-fusion elementwise | flops 128 | bytes 1024 | tf_op jit(solution)/shard_map/convert_element_type | solution.py:598
  1.4 0.1 copy.23
  1.5 0.8 %copy.21 = s32[1,1,8,4,4]{4,3,2,1,0:T(4,128)S(1)} copy(s32[1,1,8,4,4]{2,4,3,1,0:T(4,128)} %param.9) | data formatting | bytes 1024 | tf_op jit(solution)/shard_map/lt | solution.py:594
  2.3 0.1 iota_compare_fusion
  2.4 0.0 copy-done.3
  2.4 0.2 compare_select_fusion
  2.6 0.2 broadcast_in_dim.24
  2.8 0.0 copy-done.1
  2.8 0.0 copy-start.2
  2.8 0.1 copy.14
  2.9 0.8 %copy-done.2 = f32[1,1,8,4,4,3,128]{6,4,5,3,2,1,0:T(4,128)S(1)} copy-done((f32[1,1,8,4,4,3,128]{6,4,5,3,2,1,0:T(4,128)S(1)}, f32[1,1,8,4,4,3,128]{6,4,5,3,2,1,0:T(4,128)}, u32[]{:S(2)}) %copy-start.2) | copy-done | bytes 196632
  3.8 0.1 copy.17
  3.8 0.1 bitcast_select_fusion
  4.0 1.0 %pad_maximum_fusion.src = f32[32,4,8,128]{3,2,1,0:T(8,128)} fusion(f32[32,4,1,128]{3,2,1,0:T(1,128)S(1)} %broadcast_in_dim.24, f32[32,4,1,128]{3,2,1,0:T(1,128)S(1)} %compare_select_fusion, f32[32,4,3,128]{3,2,1,0:T(4,128)S(1)} %bitcast_select_fusion, f32[32,4,3,128]{3,2,1,0:T(4,128)S(1)} %bitcast.8), kind=kLoop, calls=%fused_computation | loop fusion | flops 393216 | bytes 1048576 | tf_op jit(solution)/shard_map/concatenate | solution.py:600
  5.0 16.2 %exchange.1.points = f32[32,4,8,128]{3,2,1,0:T(8,128)} custom-call(f32[32,4,8,128]{3,2,1,0:T(8,128)} %pad_maximum_fusion.src), custom_call_target="tpu_custom_call" | custom-call | tf_op jit(solution)/shard_map/exchange/pallas_call | solution.py:506
  21.2 3.4 %convert_reduce_fusion = s32[32,4]{1,0:T(8,128)S(1)} fusion(f32[32,4,8,128]{3,2,1,0:T(8,128)} %exchange.1.points), kind=kLoop, calls=%fused_computation.4 | loop fusion | flops 128 | bytes 1024 | tf_op jit(solution)/shard_map/convert_element_type | solution.py:610
  24.6 0.1 convert_element_type.21.ids
  24.7 0.0 copy-start
  24.7 1.0 %copy-done = f32[32,4,8,128]{3,2,1,0:T(8,128)S(1)} copy-done((f32[32,4,8,128]{3,2,1,0:T(8,128)S(1)}, f32[32,4,8,128]{3,2,1,0:T(8,128)}, u32[]{:S(2)}) %copy-start) | copy-done | bytes 524312
  25.7 8.3 %splat.1.g = f32[4,16,16,128]{3,2,1,0:T(8,128)S(1)} custom-call(s32[128]{0:T(128)S(1)} %convert_element_type.21.ids, f32[32,4,8,128]{3,2,1,0:T(8,128)S(1)} %copy-done), custom_call_target="tpu_custom_call" | custom-call | tf_op jit(solution)/shard_map/splat/pallas_call | solution.py:577
  34.0 0.7 slice_bitcast_fusion
  34.6 33.4 %cycle.1 = f32[16,16,128]{2,1,0:T(8,128)S(1)} custom-call(f32[4,16,16,128]{3,2,1,0:T(8,128)S(1)} %splat.1.g), custom_call_target="tpu_custom_call" | custom-call | tf_op jit(solution)/shard_map/cycle/pallas_call | solution.py:443
  68.1 0.7 copy.26
Async XLA Ops:
  0.6 1.8 %copy-start.3 = (f32[1,1,8,4,4,128]{5,4,3,2,1,0:T(4,128)S(1)}, f32[1,1,8,4,4,128]{5,4,3,2,1,0:T(4,128)}, u32[]{:S(2)}) copy-start(f32[1,1,8,4,4,128]{5,4,3,2,1,0:T(4,128)} %param.7) | copy-start | bytes 196612
  0.6 2.2 %copy-start.1 = (f32[1,1,8,4,4,3,128]{6,4,5,3,2,1,0:T(4,128)S(1)}, f32[1,1,8,4,4,3,128]{6,4,5,3,2,1,0:T(4,128)}, u32[]{:S(2)}) copy-start(f32[1,1,8,4,4,3,128]{6,4,5,3,2,1,0:T(4,128)} %param.5) | copy-start | bytes 589828
  2.8 0.9 %copy-start.2 = (f32[1,1,8,4,4,3,128]{6,4,5,3,2,1,0:T(4,128)S(1)}, f32[1,1,8,4,4,3,128]{6,4,5,3,2,1,0:T(4,128)}, u32[]{:S(2)}) copy-start(f32[1,1,8,4,4,3,128]{6,4,5,3,2,1,0:T(4,128)} %param.6) | copy-start | bytes 589828
  24.7 1.0 %copy-start = (f32[32,4,8,128]{3,2,1,0:T(8,128)S(1)}, f32[32,4,8,128]{3,2,1,0:T(8,128)}, u32[]{:S(2)}) copy-start(f32[32,4,8,128]{3,2,1,0:T(8,128)} %exchange.1.points) | copy-start | bytes 1572868

commit v3 on v2

--- a/solution.py
+++ b/solution.py
@@ -141,7 +141,7 @@
 
 
 def cycle_kernel(
-    ns, nb, g, out,
+    ns, nb, g, rho, out,
     vxp, vyp, rhop, fp, ua, ub, wf, ws, rt,
     rho1p, f1p, u1a, u1b, wf1, ws1, rt1, pr,
     gsend, gath, f2g, rho2g, u2p, c2,
@@ -201,7 +201,7 @@
     ]
     vxp[1:17] = g[0]
     vyp[:, 8:24] = g[1]
-    rhop[4:20, 8:24] = g[3]
+    rhop[4:20, 8:24] = rho[...]
     for halo in (rho_halo, f_halo, rho1_halo, f1_halo):
         halo.clear_rim()
 
@@ -244,7 +244,7 @@
 
     @planes(0, 8)
     def _(x):
-        rt[x, 8:24] = g[3, 2 * x] + g[3, 2 * x + 1]
+        rt[x, 8:24] = rho[2 * x] + rho[2 * x + 1]
 
     pool_to_1(rho1p)
     rho1_halo.start()
@@ -435,7 +435,7 @@
     pltpu.make_async_copy(every, every, gsend_sem).wait()
 
 
-def cycle(grid):
+def cycle(vectors, density):
     ns, nb = lax.axis_size("space"), lax.axis_size("sub")
     n = ns * nb
     vm = lambda *shape: pltpu.VMEM(shape, jnp.float32)
@@ -443,7 +443,7 @@
     return pl.pallas_call(
         functools.partial(cycle_kernel, ns, nb),
         out_shape=jax.ShapeDtypeStruct((CX, CY, CZ), jnp.float32),
-        in_specs=[pl.BlockSpec(memory_space=pltpu.VMEM)],
+        in_specs=[pl.BlockSpec(memory_space=pltpu.VMEM)] * 2,
         out_specs=pl.BlockSpec(memory_space=pltpu.VMEM),
         scratch_shapes=[
             vm(18, 16, 128), vm(16, 32, 128), vm(*fine), vm(*fine), vm(*fine), vm(*fine),
@@ -461,11 +461,15 @@
             collective_id=0, has_side_effects=True, vmem_limit_bytes=48 * 1024 * 1024
         ),
         name="cycle",
-    )(grid)
-
-
-def exchange_kernel(ns, nb, src, dst, send_sem, recv_sem, own_sem):
+    )(vectors, density)
+
+
+def exchange_kernel(
+    ns, nb, points_hbm, meta_hbm, parts, meta_out,
+    points, meta, point_send, point_recv, meta_send, meta_recv, own_sem,
+):
     n = ns * nb
+    tiles = points_hbm.shape[2]
     me = lax.axis_index("space") * nb + lax.axis_index("sub")
     barrier = pltpu.get_barrier_semaphore()
 
@@ -478,75 +482,136 @@
         return carry
 
     lax.fori_loop(1, n, greet, 0)
-    own = pltpu.make_async_copy(src.at[me], dst.at[me], own_sem)
-    own.start()
+    own_points = pltpu.make_async_copy(points_hbm.at[me], points.at[0], own_sem.at[0])
+    own_meta = pltpu.make_async_copy(meta_hbm.at[me], meta.at[0], own_sem.at[1])
+    own_points.start()
+    own_meta.start()
     pl.semaphore_wait(barrier, n - 1)
 
-    def tell(k, carry):
+    def copies(k):
         peer, place = where(k)
-        pltpu.make_async_remote_copy(
-            src_ref=src.at[peer],
-            dst_ref=dst.at[me],
-            send_sem=send_sem,
-            recv_sem=recv_sem,
+        one = pltpu.make_async_remote_copy(
+            src_ref=meta_hbm.at[peer],
+            dst_ref=meta.at[k],
+            send_sem=meta_send.at[k],
+            recv_sem=meta_recv.at[k],
             device_id=place,
             device_id_type=MESH,
-        ).start()
+        )
+        two = pltpu.make_async_remote_copy(
+            src_ref=points_hbm.at[peer],
+            dst_ref=points.at[k],
+            send_sem=point_send.at[k],
+            recv_sem=point_recv.at[k],
+            device_id=place,
+            device_id_type=MESH,
+        )
+        return one, two
+
+    def tell(k, carry):
+        for copy in copies(k):
+            copy.start()
         return carry
 
     lax.fori_loop(1, n, tell, 0)
-    own.wait()
-    every = dst.at[pl.ds(0, n - 1)]
-    pltpu.make_async_copy(every, every, recv_sem).wait()
-    pltpu.make_async_copy(every, every, send_sem).wait()
-
-
-def exchange(packed):
-    ns, nb = lax.axis_size("space"), lax.axis_size("sub")
-    return pl.pallas_call(
-        functools.partial(exchange_kernel, ns, nb),
-        out_shape=jax.ShapeDtypeStruct(packed.shape, jnp.float32),
-        in_specs=[pl.BlockSpec(memory_space=pl.ANY)],
-        out_specs=pl.BlockSpec(memory_space=pl.ANY),
-        scratch_shapes=[pltpu.SemaphoreType.DMA] * 3,
-        compiler_params=pltpu.CompilerParams(collective_id=1, has_side_effects=True),
-        name="exchange",
-    )(packed)
-
-
-def splat_kernel(ids, points, grid, acc):
-    peers, tiles = points.shape[0], points.shape[1]
-    acc[...] = jnp.zeros_like(acc)
+
     centers = lax.broadcasted_iota(jnp.int32, (BRICK, 128), 0).astype(jnp.float32) + 0.5
+    slot = lax.broadcasted_iota(jnp.int32, (1, 128), 1)
+    left = lax.broadcasted_iota(jnp.int32, (64, 128), 1) < 64
 
     def split(value):
         high = value.astype(jnp.bfloat16)
         low = (value - high.astype(jnp.float32)).astype(jnp.bfloat16)
         return jnp.concatenate([high, low], axis=0)
 
-    def one_tile(p, t):
-        rows = points[p, t]
-        wx, wy, wz = (
-            jnp.maximum(0.0, 1.0 - jnp.abs(rows[d : d + 1] - centers)) for d in range(3)
+    def factors(k, t):
+        row = lambda feature: points[k, feature, t : t + 1, :]
+        live = slot < meta[k, :, tiles + t : tiles + t + 1]
+        wx, wy, wz = (jnp.maximum(0.0, 1.0 - jnp.abs(row(d) - centers)) for d in range(3))
+        planar = jnp.concatenate([wx[i : i + 1] * wy for i in range(BRICK)], axis=0)
+        loaded = jnp.concatenate(
+            [jnp.where(live, row(3 + c), 0.0) * wz for c in range(4)], axis=0
         )
-        planar = jnp.concatenate([wx[i : i + 1] * wy for i in range(BRICK)], axis=0)
-        loaded = jnp.concatenate([rows[3 + c : 4 + c] * wz for c in range(4)], axis=0)
-        full = lax.dot_general(
-            split(planar),
-            split(loaded),
-            (((1,), (1,)), ((), ())),
-            preferred_element_type=jnp.float32,
-        )
-        return full[0:64] + full[64:128]
+        return split(planar), split(loaded)
+
+    def splat(k):
+        for pair in range(tiles // 2):
+            a, b = factors(k, 2 * pair), factors(k, 2 * pair + 1)
+            loaded = jnp.concatenate([a[1], b[1]], axis=0)
+            first, second = (
+                lax.dot_general(
+                    planar, loaded, (((1,), (1,)), ((), ())), preferred_element_type=jnp.float32
+                )
+                for planar in (a[0], b[0])
+            )
+            first = first[0:64] + first[64:128]
+            second = second[0:64] + second[64:128]
+            parts[k, pair] = jnp.where(left, first, second)
+
+    own_meta.wait()
+    own_points.wait()
+    splat(0)
+
+    def arrive(k, carry):
+        one, two = copies(k)
+        one.wait_recv()
+        two.wait_recv()
+        splat(k)
+        return carry
+
+    lax.fori_loop(1, n, arrive, 0)
+    meta_out[...] = meta[...]
+
+    def sent(k, carry):
+        for copy in copies(k):
+            copy.wait_send()
+        return carry
+
+    lax.fori_loop(1, n, sent, 0)
+
+
+def exchange(points, meta):
+    ns, nb = lax.axis_size("space"), lax.axis_size("sub")
+    n, tiles = points.shape[0], points.shape[2]
+    vmem = pl.BlockSpec(memory_space=pltpu.VMEM)
+    return pl.pallas_call(
+        functools.partial(exchange_kernel, ns, nb),
+        out_shape=(
+            jax.ShapeDtypeStruct((n, tiles // 2, 64, 128), jnp.float32),
+            jax.ShapeDtypeStruct(meta.shape, jnp.int32),
+        ),
+        in_specs=[pl.BlockSpec(memory_space=pl.ANY)] * 2,
+        out_specs=(vmem, vmem),
+        scratch_shapes=[
+            pltpu.VMEM(points.shape, jnp.float32),
+            pltpu.VMEM(meta.shape, jnp.int32),
+            pltpu.SemaphoreType.DMA((n,)),
+            pltpu.SemaphoreType.DMA((n,)),
+            pltpu.SemaphoreType.DMA((n,)),
+            pltpu.SemaphoreType.DMA((n,)),
+            pltpu.SemaphoreType.DMA((2,)),
+        ],
+        compiler_params=pltpu.CompilerParams(
+            collective_id=1, has_side_effects=True, vmem_limit_bytes=48 * 1024 * 1024
+        ),
+        name="exchange",
+    )(points, meta)
+
+
+def gather_kernel(meta, parts, grid, density, acc):
+    n, pairs = parts.shape[0], parts.shape[1]
+    acc[...] = jnp.zeros_like(acc)
+    left = lax.broadcasted_iota(jnp.int32, (64, 128), 1) < 64
 
     def one_peer(p, carry):
-        parts = [one_tile(p, t) for t in range(tiles)]
-        for t in range(tiles):
-            brick = ids[p * tiles + t]
-            acc[brick, :, 0:64] = acc[brick, :, 0:64] + parts[t]
+        for pair in range(pairs):
+            part = parts[p, pair]
+            first, second = meta[p, 0, 2 * pair], meta[p, 0, 2 * pair + 1]
+            acc[first] = acc[first] + jnp.where(left, part, 0.0)
+            acc[second] = acc[second] + jnp.where(left, 0.0, part)
         return carry
 
-    lax.fori_loop(0, peers, one_peer, 0, unroll=2)
+    lax.fori_loop(0, n, one_peer, 0, unroll=2)
 
     group = lax.broadcasted_iota(jnp.int32, (BRICK, 128), 1) // BRICK
     nz = CZ // BRICK
@@ -558,6 +623,7 @@
             turned = []
             for bz in range(nz):
                 part = acc[column * nz + bz, pl.ds(pl.multiple_of(8 * i, 8), 8), :]
+                part = part + pltpu.roll(part, 64, 1)
                 part = part + pltpu.roll(part, 96, 1)
                 turned.append(pltpu.roll(part, 8 * bz, 1) if bz else part)
             for c in range(4):
@@ -566,50 +632,50 @@
                     value = jnp.where(group == (bz + c) % nz, turned[bz], value)
                 if c:
                     value = pltpu.roll(value, 128 - 8 * c, 1)
-                grid[c, BRICK * bx + i, BRICK * by : BRICK * by + BRICK, :] = value
+                if c < 3:
+                    grid[c, BRICK * bx + i, BRICK * by : BRICK * by + BRICK, :] = value
+                else:
+                    density[BRICK * bx + i, BRICK * by : BRICK * by + BRICK, :] = value
             return carry
 
         lax.fori_loop(0, BRICK, one_row, 0, unroll=2)
 
 
-def splat(ids, points):
+def gather(meta, parts):
     bricks = CX // BRICK * (CY // BRICK) * (CZ // BRICK)
+    vmem = pl.BlockSpec(memory_space=pltpu.VMEM)
     return pl.pallas_call(
-        splat_kernel,
-        out_shape=jax.ShapeDtypeStruct((4, CX, CY, CZ), jnp.float32),
-        in_specs=[
-            pl.BlockSpec(memory_space=pltpu.SMEM),
-            pl.BlockSpec(memory_space=pltpu.VMEM),
-        ],
-        out_specs=pl.BlockSpec(memory_space=pltpu.VMEM),
+        gather_kernel,
+        out_shape=(
+            jax.ShapeDtypeStruct((3, CX, CY, CZ), jnp.float32),
+            jax.ShapeDtypeStruct((CX, CY, CZ), jnp.float32),
+        ),
+        in_specs=[pl.BlockSpec(memory_space=pltpu.SMEM), vmem],
+        out_specs=(vmem, vmem),
         scratch_shapes=[pltpu.VMEM((bricks, 64, 128), jnp.float32)],
         compiler_params=pltpu.CompilerParams(vmem_limit_bytes=48 * 1024 * 1024),
-        name="splat",
-    )(ids, points)
+        name="gather",
+    )(meta, parts)
 
 
 def on_device(offsets, normals, density, tile_brick, tile_count):
-    devices = lax.axis_size("space") * lax.axis_size("sub")
+    n = lax.axis_size("space") * lax.axis_size("sub")
     tiles, slots = offsets.shape[4], offsets.shape[6]
-    live = lax.broadcasted_iota(jnp.int32, (devices, tiles, 1, slots), 3) < tile_count.reshape(
-        devices, tiles, 1, 1
+    by_feature = lambda a: a.reshape(n, tiles, 3, slots).transpose(0, 2, 1, 3)
+    points = jnp.concatenate(
+        [by_feature(offsets), by_feature(normals), density.reshape(n, 1, tiles, slots)], axis=1
     )
-    ids = jnp.broadcast_to(
-        tile_brick.reshape(devices, tiles, 1, 1).astype(jnp.float32), (devices, tiles, 1, slots)
-    )
-    packed = jnp.concatenate(
+    meta = jnp.concatenate(
         [
-            offsets.reshape(devices, tiles, 3, slots),
-            jnp.where(live, normals.reshape(devices, tiles, 3, slots), 0.0),
-            jnp.where(live, density.reshape(devices, tiles, 1, slots), 0.0),
-            ids,
+            tile_brick.reshape(n, 1, tiles),
+            tile_count.reshape(n, 1, tiles),
+            jnp.zeros((n, 1, 128 - 2 * tiles), jnp.int32),
         ],
         axis=2,
     )
-    points = exchange(packed)
-    bricks = points[:, :, 7, 0].astype(jnp.int32).reshape(-1)
-    grid = splat(bricks, points)
-    return (cycle(grid), grid[3])
+    parts, meta = exchange(points, meta)
+    vectors, density_field = gather(meta, parts)
+    return (cycle(vectors, density_field), density_field)
 
 
 def solution(mesh):

time: 69 us -> 66 us (0.957)
  other arithmetic: 5.57 us -> 1.26 us
  Pallas kernels: 57.9 us -> 60.6 us
  local copies, waits for them, and re-layouts: 4.56 us -> 3.23 us
    pallas_call x2, Pallas kernels: 24.4 us -> 29 us  [the longest x1 21.9 us: exchange(): pl.pallas_call(functools.partial(exchange_kernel, ns, nb), out_shape=(jax...]
    convert_element_type x2 -> x0, other arithmetic: 4.13 us -> none  [the longest x1 3.39 us: on_device(): bricks = points[:, :, 7, 0].astype(jnp.int32).reshape(-1)]
    pallas_call x1, Pallas kernels: 33.4 us -> 31.6 us  [cycle(): pl.pallas_call(functools.partial(cycle_kernel, ns, nb), out_shape=jax.Sha...]
    reshape x0 -> x2, local copies, waits for them, and re-layouts: none -> 1.59 us  [the longest x1 0.79 us: on_device(): tile_brick.reshape(n, 1, tiles)]
    unnamed x11 -> x3, local copies, waits for them, and re-layouts: 2.69 us -> 1.56 us
    lt x1 -> x0, local copies, waits for them, and re-layouts: 0.79 us -> none  [on_device(): lax.broadcasted_iota(jnp.int32, (devices, tiles, 1, slots), 3)]
where the time goes in v3:
time: 66 us; the launch traced here: 65.8 us
  Pallas kernels  60.6 us (92%)
  local copies, waits for them, and re-layouts  3.23 us (5%)
  other arithmetic  1.26 us (2%)
  between operations  0.67 us (1%)
    pallas_call x1, Pallas kernels, cycle(): pl.pallas_call(functools.partial(cycle_kernel, ns, nb), out_shape=jax.Sha...  31.6 us
    pallas_call x1, Pallas kernels, exchange(): pl.pallas_call(functools.partial(exchange_kernel, ns, nb), out_shape=(jax...  21.9 us
    pallas_call x1, Pallas kernels, gather(): pl.pallas_call(gather_kernel, out_shape=(jax.ShapeDtypeStruct((3, CX, CY,...  7.15 us
    unnamed x3, local copies, waits for them, and re-layouts  1.56 us

profile of v3, /device:TPU:0, one launch (start us, length us, event | category | flops | bytes accessed | tf_op | source)
XLA Modules:
  0.0 65.8 jit_solution(889191097537337829)
XLA Ops:
  0.6 0.1 pad.2.clone
  0.7 0.8 %copy.15 = s32[1,1,8,4,4]{4,3,2,1,0:T(4,128)S(1)} copy(s32[1,1,8,4,4]{2,4,3,1,0:T(4,128)} %param.8) | data formatting | bytes 1024 | tf_op jit(solution)/shard_map/reshape | solution.py:670
  1.5 0.8 %copy.16 = s32[1,1,8,4,4]{4,3,2,1,0:T(4,128)S(1)} copy(s32[1,1,8,4,4]{2,4,3,1,0:T(4,128)} %param.9) | data formatting | bytes 1024 | tf_op jit(solution)/shard_map/reshape | solution.py:671
  2.3 0.1 add_add_fusion.meta_hbm
  2.4 1.2 %pad_maximum_fusion.points_hbm = f32[32,7,4,128]{3,2,1,0:T(4,128)S(1)} fusion(f32[32,1,4,128]{3,2,1,0:T(4,128)} %bitcast.11, f32[32,3,4,128]{3,2,1,0:T(4,128)} %bitcast.9, f32[32,3,4,128]{3,2,1,0:T(4,128)} %bitcast.10), kind=kLoop, calls=%fused_computation | loop fusion | flops 229376 | bytes 917504 | tf_op jit(solution)/shard_map/concatenate | solution.py:665
  3.6 21.9 %exchange.1 = (f32[32,2,64,128]{3,2,1,0:T(8,128)S(1)}, s32[32,1,128]{2,1,0:T(1,128)S(1)}) custom-call(f32[32,7,4,128]{3,2,1,0:T(4,128)S(1)} %pad_maximum_fusion.points_hbm, s32[32,1,128]{2,1,0:T(1,128)S(1)} %add_add_fusion.meta_hbm), custom_call_target="tpu_custom_call" | custom-call | tf_op jit(solution)/shard_map/exchange/pallas_call | solution.py:577
  25.5 7.2 %gather.1 = (f32[3,16,16,128]{3,2,1,0:T(8,128)S(1)}, f32[16,16,128]{2,1,0:T(8,128)}) custom-call(s32[32,1,128]{2,1,0:T(1,128)S(1)} %get-tuple-element.6.meta, f32[32,2,64,128]{3,2,1,0:T(8,128)S(1)} %get-tuple-element.7.parts), custom_call_target="tpu_custom_call" | custom-call | tf_op jit(solution)/shard_map/gather/pallas_call | solution.py:647
  32.6 0.0 copy-start
  32.6 0.9 %copy-done = f32[16,16,128]{2,1,0:T(8,128)S(1)} copy-done((f32[16,16,128]{2,1,0:T(8,128)S(1)}, f32[16,16,128]{2,1,0:T(8,128)}, u32[]{:S(2)}) %copy-start) | copy-done | bytes 131096
  33.5 31.6 %cycle.1 = f32[16,16,128]{2,1,0:T(8,128)S(1)} custom-call(f32[3,16,16,128]{3,2,1,0:T(8,128)S(1)} %get-tuple-element.8.g, f32[16,16,128]{2,1,0:T(8,128)S(1)} %copy-done), custom_call_target="tpu_custom_call" | custom-call | tf_op jit(solution)/shard_map/cycle/pallas_call | solution.py:443
  65.1 0.7 %copy.20 = f32[16,16,128]{2,1,0:T(8,128)} copy(f32[16,16,128]{2,1,0:T(8,128)S(1)} %cycle.1) | data formatting | bytes 262144
  (1 shorter events, 0.0 us)
Async XLA Ops:
  32.6 0.9 %copy-start = (f32[16,16,128]{2,1,0:T(8,128)S(1)}, f32[16,16,128]{2,1,0:T(8,128)}, u32[]{:S(2)}) copy-start(f32[16,16,128]{2,1,0:T(8,128)} %get-tuple-element.13.rho) | copy-start | bytes 393220

commit v4 on v3

--- a/solution.py
+++ b/solution.py
@@ -1,4 +1,5 @@
 import functools
+import math
 
 import jax
 import jax.numpy as jnp
@@ -32,6 +33,15 @@
 
 def grid_iota(shape):
     return lax.broadcasted_iota(jnp.int32, shape, 0), lax.broadcasted_iota(jnp.int32, shape, 1)
+
+
+def modulo(value, size):
+    return value & (size - 1) if size & (size - 1) == 0 else value % size
+
+
+def over(value, size):
+    shift = size.bit_length() - 1
+    return value >> shift if size & (size - 1) == 0 else value // size
 
 
 def one_where(mask, value=1.0):
@@ -59,7 +69,7 @@
 def flat_neighbours(u, xs, zl, yl):
     row, lane = grid_iota(u.shape)
     rows = u.shape[0]
-    xi, zi, yi = row % xs, lane % zl, lane // zl
+    xi, zi, yi = modulo(row, xs), modulo(lane, zl), over(lane, zl)
     total = jnp.where(zi < zl - 1, pltpu.roll(u, 127, 1), 0.0)
     total = total + jnp.where(zi > 0, pltpu.roll(u, 1, 1), 0.0)
     total = total + jnp.where(xi < xs - 1, pltpu.roll(u, rows - 1, 0), 0.0)
@@ -129,7 +139,9 @@
             pl.when(self.has(dx, dy))(copy.wait_send)
 
 
-def planes(start, stop, unroll=2):
+def planes(start, stop, unroll=None):
+    unroll = unroll or stop - start
+
     def wrap(body):
         def step(x, carry):
             body(x)
@@ -141,7 +153,7 @@
 
 
 def cycle_kernel(
-    ns, nb, g, rho, out,
+    ns, nb, g, out,
     vxp, vyp, rhop, fp, ua, ub, wf, ws, rt,
     rho1p, f1p, u1a, u1b, wf1, ws1, rt1, pr,
     gsend, gath, f2g, rho2g, u2p, c2,
@@ -201,7 +213,7 @@
     ]
     vxp[1:17] = g[0]
     vyp[:, 8:24] = g[1]
-    rhop[4:20, 8:24] = rho[...]
+    rhop[4:20, 8:24] = g[3]
     for halo in (rho_halo, f_halo, rho1_halo, f1_halo):
         halo.clear_rim()
 
@@ -222,16 +234,16 @@
         vyp[:, 24:32] = jnp.zeros((16, 8, 128), jnp.float32)
 
     zr, zc = grid_iota((128, 128))
-    pool_z = one_where(zr // 2 == zc, 0.125)
+    pool_z = one_where(over(zr, 2) == zc, 0.125)
 
     def pool_to_1(dst):
         pooled = rt[:, pl.ds(8, 8, stride=2), :] + rt[:, pl.ds(9, 8, stride=2), :]
         dst[4:12, 8:16] = dot(pooled.reshape(64, 128), pool_z).reshape(8, 8, 128)
 
-    pool_lanes = one_where(zr // 2 == zc % 32, 0.125)
+    pool_lanes = one_where(over(zr, 2) == modulo(zc, 32), 0.125)
     prow = lax.broadcasted_iota(jnp.int32, (4, 8, 128), 1)
     plane_lane = lax.broadcasted_iota(jnp.int32, (4, 8, 128), 2)
-    pick_rows = plane_lane // 32 == prow // 2
+    pick_rows = over(plane_lane, 32) == over(prow, 2)
 
     def pool_to_2(value):
         spread = dot(value.reshape(32, 128), pool_lanes).reshape(4, 8, 128)
@@ -244,7 +256,7 @@
 
     @planes(0, 8)
     def _(x):
-        rt[x, 8:24] = rho[2 * x] + rho[2 * x + 1]
+        rt[x, 8:24] = g[3, 2 * x] + g[3, 2 * x + 1]
 
     pool_to_1(rho1p)
     rho1_halo.start()
@@ -307,7 +319,7 @@
 
     sweeps(ua, ub, wf, ws, 1.0, 2, 22, True)
 
-    @planes(0, 8, 1)
+    @planes(0, 8)
     def _(x):
         parts = []
         for k in range(2):
@@ -330,7 +342,7 @@
     u1b[0] = jnp.zeros((24, 128), jnp.float32)
     u1b[15] = jnp.zeros((24, 128), jnp.float32)
 
-    @planes(0, 4, 1)
+    @planes(0, 4)
     def _(x):
         parts = []
         for k in range(2):
@@ -358,9 +370,24 @@
     gath[mine] = gsend[...]
     u2p[...] = jnp.zeros_like(u2p)
     every = gath.at[pl.ds(0, n - 1)]
-    pltpu.make_async_copy(every, every, grecv_sem).wait()
     x2, x3 = ns * 4, ns * 2
     rows2, rows3 = nb * x2, nb * x3
+    r3, r2 = grid_iota((rows3, rows2))
+    pool_rows = one_where(over(r2, 2) == r3)
+    t2, t3 = grid_iota((rows2, rows3))
+    grow_rows = one_where(over(t2, 2) == t3)
+    pool_l = one_where(over(zr, 64) * 16 + over(modulo(zr, 32), 2) == zc, 0.125)
+    grow_l = one_where(over(zc, 64) * 16 + over(modulo(zc, 32), 2) == zr)
+    grow_z = one_where(zr == over(zc, 2))
+    q0, q1 = grid_iota((128, 512))
+    q_lane = modulo(q1, 128)
+    grow_q = one_where(
+        jnp.logical_and(
+            over(q0, 32) == over(q1, 128),
+            jnp.logical_and(modulo(q0, 32) == over(q_lane, 2), q_lane < 64),
+        )
+    )
+    pltpu.make_async_copy(every, every, grecv_sem).wait()
     for b in range(nb):
         for s in range(ns):
             f2g[b, 4 * s : 4 * s + 4] = gath[b * ns + s, 0:4]
@@ -369,12 +396,6 @@
     rho2 = rho2g[...].reshape(rows2, 128)
     diag2 = 0.375 + screen_weight * rho2
     w2 = relax_weight / diag2
-    r3, r2 = grid_iota((rows3, rows2))
-    pool_rows = one_where(r2 // 2 == r3)
-    t2, t3 = grid_iota((rows2, rows3))
-    grow_rows = one_where(t2 // 2 == t3)
-    pool_l = one_where((zr // 64) * 16 + (zr % 32) // 2 == zc, 0.125)
-    grow_l = one_where((zc // 64) * 16 + (zc % 32) // 2 == zr)
     rho3 = dot(dot(pool_rows, rho2), pool_l)
     lane3 = grid_iota((rows3, 128))[1]
     w3 = jnp.where(lane3 < 32, relax_weight / (0.09375 + screen_weight * rho3), 0.0)
@@ -395,10 +416,6 @@
     u2p[1 : nb + 1, 8 : 8 + x2] = u2.reshape(nb, x2, 128)
 
     near = [u2p[sb + o, pl.ds(4 * sp + 6, 8), :] for o in range(3)]
-    q0, q1 = grid_iota((128, 512))
-    grow_q = one_where(
-        jnp.logical_and(q0 // 32 == q1 // 128, jnp.logical_and(q0 % 32 == (q1 % 128) // 2, q1 % 128 < 64))
-    )
     fan = dot(jnp.concatenate(near, axis=0), grow_q)
     order = [(0, 2), (0, 3), (1, 0), (1, 1), (1, 2), (1, 3), (2, 0), (2, 1)]
     for at, (o, j) in enumerate(order):
@@ -410,10 +427,9 @@
                 u1b[2 * i + k, rows, :] = u1b[2 * i + k, rows, :] + c2[i]
     sweeps(u1b, u1a, wf1, ws1, 0.25, 2, 14, False)
     sweeps(u1a, u1b, wf1, ws1, 0.25, 3, 13, False)
-    grow_z = one_where(zr == zc // 2)
     pr[...] = dot(u1b[3:13].reshape(240, 128), grow_z).reshape(10, 24, 128)
 
-    @planes(0, 10, 1)
+    @planes(0, 10)
     def _(i):
         for k in range(2):
             for m in range(2):
@@ -435,7 +451,7 @@
     pltpu.make_async_copy(every, every, gsend_sem).wait()
 
 
-def cycle(vectors, density):
+def cycle(grid):
     ns, nb = lax.axis_size("space"), lax.axis_size("sub")
     n = ns * nb
     vm = lambda *shape: pltpu.VMEM(shape, jnp.float32)
@@ -443,7 +459,7 @@
     return pl.pallas_call(
         functools.partial(cycle_kernel, ns, nb),
         out_shape=jax.ShapeDtypeStruct((CX, CY, CZ), jnp.float32),
-        in_specs=[pl.BlockSpec(memory_space=pltpu.VMEM)] * 2,
+        in_specs=[pl.BlockSpec(memory_space=pltpu.VMEM)],
         out_specs=pl.BlockSpec(memory_space=pltpu.VMEM),
         scratch_shapes=[
             vm(18, 16, 128), vm(16, 32, 128), vm(*fine), vm(*fine), vm(*fine), vm(*fine),
@@ -461,7 +477,7 @@
             collective_id=0, has_side_effects=True, vmem_limit_bytes=48 * 1024 * 1024
         ),
         name="cycle",
-    )(vectors, density)
+    )(grid)
 
 
 def exchange_kernel(
@@ -548,18 +564,27 @@
             second = second[0:64] + second[64:128]
             parts[k, pair] = jnp.where(left, first, second)
 
+    width = math.gcd(n, 4)
+
+    def land(k):
+        for copy in copies(k):
+            copy.wait_recv()
+
     own_meta.wait()
     own_points.wait()
-    splat(0)
-
-    def arrive(k, carry):
-        one, two = copies(k)
-        one.wait_recv()
-        two.wait_recv()
+    for k in range(1, width):
+        land(k)
+    for k in range(width):
         splat(k)
+
+    def arrive(group, carry):
+        for k in range(width):
+            land(group * width + k)
+        for k in range(width):
+            splat(group * width + k)
         return carry
 
-    lax.fori_loop(1, n, arrive, 0)
+    lax.fori_loop(1, n // width, arrive, 0)
     meta_out[...] = meta[...]
 
     def sent(k, carry):
@@ -598,17 +623,18 @@
     )(points, meta)
 
 
-def gather_kernel(meta, parts, grid, density, acc):
+def gather_kernel(meta, parts, grid, density, acc, acd):
     n, pairs = parts.shape[0], parts.shape[1]
     acc[...] = jnp.zeros_like(acc)
-    left = lax.broadcasted_iota(jnp.int32, (64, 128), 1) < 64
+    acd[...] = jnp.zeros_like(acd)
+    left = lax.broadcasted_iota(jnp.int32, (BRICK, 128), 1) < 64
 
     def one_peer(p, carry):
         for pair in range(pairs):
             part = parts[p, pair]
             first, second = meta[p, 0, 2 * pair], meta[p, 0, 2 * pair + 1]
-            acc[first] = acc[first] + jnp.where(left, part, 0.0)
-            acc[second] = acc[second] + jnp.where(left, 0.0, part)
+            acc[first] = acc[first] + part
+            acd[second] = acd[second] + part
         return carry
 
     lax.fori_loop(0, n, one_peer, 0, unroll=2)
@@ -620,25 +646,24 @@
         bx, by = column // (CY // BRICK), column % (CY // BRICK)
 
         def one_row(i, carry):
-            turned = []
+            values = [None] * 4
+            rows = pl.ds(pl.multiple_of(8 * i, 8), 8)
             for bz in range(nz):
-                part = acc[column * nz + bz, pl.ds(pl.multiple_of(8 * i, 8), 8), :]
+                brick = column * nz + bz
+                part = jnp.where(left, acc[brick, rows, :], acd[brick, rows, :])
                 part = part + pltpu.roll(part, 64, 1)
                 part = part + pltpu.roll(part, 96, 1)
-                turned.append(pltpu.roll(part, 8 * bz, 1) if bz else part)
+                part = pltpu.roll(part, 8 * bz, 1) if bz else part
+                for c in range(4):
+                    values[c] = jnp.where(group == (bz + c) % nz, part, values[c]) if bz else part
             for c in range(4):
-                value = turned[0]
-                for bz in range(1, nz):
-                    value = jnp.where(group == (bz + c) % nz, turned[bz], value)
-                if c:
-                    value = pltpu.roll(value, 128 - 8 * c, 1)
-                if c < 3:
-                    grid[c, BRICK * bx + i, BRICK * by : BRICK * by + BRICK, :] = value
-                else:
+                value = pltpu.roll(values[c], 128 - 8 * c, 1) if c else values[c]
+                grid[c, BRICK * bx + i, BRICK * by : BRICK * by + BRICK, :] = value
+                if c == 3:
                     density[BRICK * bx + i, BRICK * by : BRICK * by + BRICK, :] = value
             return carry
 
-        lax.fori_loop(0, BRICK, one_row, 0, unroll=2)
+        lax.fori_loop(0, BRICK, one_row, 0, unroll=4)
 
 
 def gather(meta, parts):
@@ -647,12 +672,12 @@
     return pl.pallas_call(
         gather_kernel,
         out_shape=(
-            jax.ShapeDtypeStruct((3, CX, CY, CZ), jnp.float32),
+            jax.ShapeDtypeStruct((4, CX, CY, CZ), jnp.float32),
             jax.ShapeDtypeStruct((CX, CY, CZ), jnp.float32),
         ),
         in_specs=[pl.BlockSpec(memory_space=pltpu.SMEM), vmem],
         out_specs=(vmem, vmem),
-        scratch_shapes=[pltpu.VMEM((bricks, 64, 128), jnp.float32)],
+        scratch_shapes=[pltpu.VMEM((bricks, 64, 128), jnp.float32)] * 2,
         compiler_params=pltpu.CompilerParams(vmem_limit_bytes=48 * 1024 * 1024),
         name="gather",
     )(meta, parts)
@@ -674,8 +699,8 @@
         axis=2,
     )
     parts, meta = exchange(points, meta)
-    vectors, density_field = gather(meta, parts)
-    return (cycle(vectors, density_field), density_field)
+    grid, density_field = gather(meta, parts)
+    return (cycle(grid), density_field)
 
 
 def solution(mesh):

time: 66 us -> 57.2 us (0.87)
  Pallas kernels: 60.6 us -> 52.7 us
  local copies, waits for them, and re-layouts: 3.23 us -> 2.32 us
    pallas_call x1, Pallas kernels: 31.6 us -> 28.4 us  [cycle(): pl.pallas_call(functools.partial(cycle_kernel, ns, nb), out_shape=jax.Sha...]
    pallas_call x1, Pallas kernels: 21.9 us -> 18.9 us  [exchange(): pl.pallas_call(functools.partial(exchange_kernel, ns, nb), out_shape=(jax...]
    pallas_call x1, Pallas kernels: 7.15 us -> 5.42 us  [gather(): pl.pallas_call(gather_kernel, out_shape=(jax.ShapeDtypeStruct((4, CX, CY,...]
    unnamed x3 -> x1, local copies, waits for them, and re-layouts: 1.56 us -> 0.66 us
where the time goes in v4:
time: 57.2 us; the launch traced here: 57 us
  Pallas kernels  52.7 us (92%)
  local copies, waits for them, and re-layouts  2.32 us (4%)
  other arithmetic  1.26 us (2%)
  between operations  0.67 us (1%)
    pallas_call x1, Pallas kernels, cycle(): pl.pallas_call(functools.partial(cycle_kernel, ns, nb), out_shape=jax.Sha...  28.4 us
    pallas_call x1, Pallas kernels, exchange(): pl.pallas_call(functools.partial(exchange_kernel, ns, nb), out_shape=(jax...  18.9 us
    pallas_call x1, Pallas kernels, gather(): pl.pallas_call(gather_kernel, out_shape=(jax.ShapeDtypeStruct((4, CX, CY,...  5.42 us
    concatenate x1, other arithmetic, on_device(): jnp.concatenate([by_feature(offsets), by_feature(normals), density.reshap...  1.16 us

profile of v4, /device:TPU:0, one launch (start us, length us, event | category | flops | bytes accessed | tf_op | source)
XLA Modules:
  0.0 57.0 jit_solution(3892038770401464434)
XLA Ops:
  0.6 0.1 pad.2.clone
  0.7 0.8 %copy.15 = s32[1,1,8,4,4]{4,3,2,1,0:T(4,128)S(1)} copy(s32[1,1,8,4,4]{2,4,3,1,0:T(4,128)} %param.8) | data formatting | bytes 1024 | tf_op jit(solution)/shard_map/reshape | solution.py:695
  1.5 0.8 %copy.16 = s32[1,1,8,4,4]{4,3,2,1,0:T(4,128)S(1)} copy(s32[1,1,8,4,4]{2,4,3,1,0:T(4,128)} %param.9) | data formatting | bytes 1024 | tf_op jit(solution)/shard_map/reshape | solution.py:696
  2.3 0.1 add_add_fusion.meta_hbm
  2.4 1.2 %pad_maximum_fusion.points_hbm = f32[32,7,4,128]{3,2,1,0:T(4,128)S(1)} fusion(f32[32,1,4,128]{3,2,1,0:T(4,128)} %bitcast.11, f32[32,3,4,128]{3,2,1,0:T(4,128)} %bitcast.9, f32[32,3,4,128]{3,2,1,0:T(4,128)} %bitcast.10), kind=kLoop, calls=%fused_computation | loop fusion | flops 229376 | bytes 917504 | tf_op jit(solution)/shard_map/concatenate | solution.py:690
  3.6 18.9 %exchange.1 = (f32[32,2,64,128]{3,2,1,0:T(8,128)S(1)}, s32[32,1,128]{2,1,0:T(1,128)S(1)}) custom-call(f32[32,7,4,128]{3,2,1,0:T(4,128)S(1)} %pad_maximum_fusion.points_hbm, s32[32,1,128]{2,1,0:T(1,128)S(1)} %add_add_fusion.meta_hbm), custom_call_target="tpu_custom_call" | custom-call | tf_op jit(solution)/shard_map/exchange/pallas_call | solution.py:602
  22.5 5.4 %gather.1 = (f32[4,16,16,128]{3,2,1,0:T(8,128)S(1)}, f32[16,16,128]{2,1,0:T(8,128)}) custom-call(s32[32,1,128]{2,1,0:T(1,128)S(1)} %get-tuple-element.6.meta, f32[32,2,64,128]{3,2,1,0:T(8,128)S(1)} %get-tuple-element.7.parts), custom_call_target="tpu_custom_call" | custom-call | tf_op jit(solution)/shard_map/gather/pallas_call | solution.py:672
  27.9 28.4 %cycle.1 = f32[16,16,128]{2,1,0:T(8,128)S(1)} custom-call(f32[4,16,16,128]{3,2,1,0:T(8,128)S(1)} %get-tuple-element.8.g), custom_call_target="tpu_custom_call" | custom-call | tf_op jit(solution)/shard_map/cycle/pallas_call | solution.py:459
  56.3 0.7 %copy.20 = f32[16,16,128]{2,1,0:T(8,128)} copy(f32[16,16,128]{2,1,0:T(8,128)S(1)} %cycle.1) | data formatting | bytes 262144
  (1 shorter events, 0.0 us)
